TPU v7x, 32 devices: a whole 2x2x4 slice. The times are simulated.
32 devices in a mesh: dom: 32 (over z, y, x, core).
Axes of the slice: x: 2, y: 2, z: 4, core: 2. Of those that a mesh axis runs over, the one named last changes fastest.
Arguments:
- element_freedom_values: float32 [9, 20, 32768], P(None, None, 'dom'), may hold values from -6 to 6
- scaled_jacobian_matrices: float32 [3, 9, 9, 32768], P(None, None, None, 'dom'), may hold values from -2 to 2
- outward_face_normals: float32 [4, 3, 32768], P(None, None, 'dom'), may hold values from -3 to 3
- largest_wave_speed: float32 [32768], P('dom'), may hold values from 0.5 to 2
- element_cluster_index: int32 [32768], P('dom'), may hold values 0 or 1
- element_new_slot: int32 [32768], P('dom'), may hold values from 0 to 36863, as said below
- neighbours: int32 [4, 32768], P(None, 'dom'), may hold values from 0 to 36607, as said below
- face_rotation_codes: int32 [4, 32768], P(None, 'dom'), may hold values from 0 to 11
- deriv_mats: float32 [3, 20, 20], replicated, may hold values from -1.25 to 1.25
- stiff_mats: float32 [3, 20, 20], replicated, may hold values from -1.25 to 1.25
- face_eval: float32 [12, 20, 16], replicated, may hold values from -1.25 to 1.25
- face_lift: float32 [4, 16, 20], replicated, may hold values from -1.5 to 1.5
Outputs:
- new_state: float32 [9, 20, 36864], P(None, None, 'dom')
Inputs may be any that keep to these rules, and one draw needn't show every extreme that they name: `element_new_slot`: one to one into slots partition * 1152 + local slot. Element 896 + j of partition d either stays at its local index or, on partitions that shed work, goes with g = j div 16 to partition (d + max(g * 4, 1)) mod 32, local slot 1024 + g * 16 + j mod 16; a partition sheds all 128 such elements or none; elements below 896 stay. Partitions 0 and 31 receive all 8 groups. `neighbours`: each names an occupied slot whose local index is below 896, on the element's own partition after migration or on one at s partitions' distance, s in -4..4 or s = 16, cyclically; at most one face of an element lies off its partition; from the elements of one partition after migration at most 32 faces name any one other partition, and partition 0 is named by exactly 32 faces from each of the nine partitions at those distances.
All inputs are finite; a program needn't handle non-finite values. No bound on the sum of `element_cluster_index` on one device may be relied on, other than what follows from the above.
Results may differ from a plain program's by a relative error of at most 0.0001.
Values sent between devices are 32-bit elements; how exact they have to be, the bound alone decides.
No kernel may reach another device: no remote copies, remote signals or barrier semaphores. Data moves between devices by JAX's collectives and lax.ppermute only.
A program may use at most 256 MiB of HBM per device.

v0:
```python
import math

import jax
import jax.numpy as jnp
from jax import lax
from jax.experimental import pallas as pl
from jax.experimental.pallas import tpu as pltpu
from jax.sharding import PartitionSpec as P

NV = 9
NB = 20
NBP = 24
NQ = 16
NORDER = 4
GROUPS = 8
CSZ = 16
KEEP = 896
PARTITION_SLOTS = 1152
REQ = 32
PARTNERS = 9
ASKS = 16
LANES = 128
WIDE = 256
BOTH = 512
ROWS = 216
JAC_END = ROWS + 4 * NV * NV
PACK = 192
MSG = 256
FAR = 384
RECORD = 640
SMALL = 24
MESSAGE1 = REQ + 8

step_fast = 0.25
exact = lax.Precision.HIGHEST
f32 = jnp.float32
bf16 = jnp.bfloat16
i32 = jnp.int32

SPEED, CLUSTER, LINK, ORIENT, OCCUPIED = 12, 13, 14, 18, 22

MOST = pltpu.CompilerParams(vmem_limit_bytes=60 << 20)
PARAMS = pltpu.CompilerParams(vmem_limit_bytes=20 << 20)


def coefficients(lower, upper):
    return [
        (upper ** (degree + 1) - lower ** (degree + 1)) / math.factorial(degree + 1)
        for degree in range(NORDER)
    ]


FIRST = coefficients(0.0, step_fast)
SECOND = coefficients(step_fast, 2.0 * step_fast)


def partner_offsets(devices):
    return [1, 2, 3, 4, -1, -2, -3, -4, devices // 2]


def packed_row(quantity, basis):
    group, member = quantity // 3, quantity % 3
    inside = 16 * member + basis if basis < 16 else 48 + 4 * member + (basis - 16)
    return 64 * group + inside


def pack_three(members):
    a, b, c = members
    tail = a[16:24] + pltpu.roll(b[16:24], 4, 0)
    return jnp.concatenate([a[:16], b[:16], c[:16], tail, c[16:24]], axis=0)


def split(values):
    high = values.astype(bf16)
    low = (values - high.astype(f32)).astype(bf16)
    return high, low


def stacked(high, low):
    return jnp.concatenate([high, low, high], axis=0)


def dot(a, b):
    return jnp.dot(a, b, preferred_element_type=f32)


def dot_last(a, b):
    return lax.dot_general(a, b, (((1,), (1,)), ((), ())), preferred_element_type=f32)


def iota(shape, axis):
    return lax.broadcasted_iota(i32, shape, axis)


def one_hot(condition):
    return jnp.where(condition, 1.0, 0.0).astype(bf16)


def make_weights(deriv, stiff, evals, lift, w_pred, w_own, w_lift, w_table, w_far, square):
    def turned(matrix, rows, columns):
        square[...] = jnp.zeros((LANES, LANES), f32)
        square[:rows, :columns] = matrix
        return square[...].T[:NBP]

    column = iota((LANES, PACK), 1) & 63
    member = jnp.where(column < 48, column >> 4, (column - 48) >> 2)
    basis = jnp.where(column < 48, column & 15, 16 + (column & 3))
    spread = one_hot(iota((LANES, PACK), 0) == jnp.where(member < 3, basis, -1))
    member = member[:NBP]
    part = iota((NBP, PACK), 1)

    def three(matrix):
        high, low = split(turned(matrix, NB, NB))
        row = jnp.where(part < 128, dot(high, spread), dot(low, spread))
        return [jnp.where(member == inner, row, 0.0) for inner in range(3)]

    blocks = []
    for axis in range(3):
        blocks += three(-deriv[axis])
    w_pred[...] = jnp.concatenate(blocks, axis=0).astype(bf16)

    own = [
        lax.dot_general(
            evals[48 * face : 48 * face + NQ, :],
            lift[face],
            (((0,), (0,)), ((), ())),
            precision=exact,
            preferred_element_type=f32,
        )
        for face in range(4)
    ]
    blocks = []
    for matrix in [stiff[axis] for axis in range(3)] + own + [own[0] + own[1] + own[2] + own[3]]:
        blocks += three(matrix if len(blocks) < 9 else -0.5 * matrix)
    w_own[...] = jnp.concatenate(blocks, axis=0).astype(bf16)

    column = iota((LANES, 144), 1)
    spread = one_hot(iota((LANES, 144), 0) == (column & 15))
    column = column[:NBP]
    block = column >> 4
    member = block - jnp.where(column >= 96, 6, jnp.where(column >= 48, 3, 0))
    every = []
    for face in range(4):
        high, low = split(turned(lift[face], NQ, NB))
        row = jnp.where(column < 96, dot(high, spread), dot(low, spread))
        rows = [jnp.where(member == inner, -0.5 * row, 0.0) for inner in range(3)]
        w_lift[face] = jnp.concatenate(rows + [-r for r in rows], axis=0).astype(bf16)
        every += rows
    w_far[...] = jnp.concatenate(every, axis=0).astype(bf16)

    basis_of = one_hot((iota((320, NB), 0) >> 4) == iota((320, NB), 1))
    keep = (iota((320, PACK), 0) & 15) == (iota((320, PACK), 1) & 15)
    code_of = one_hot((iota((PACK, 16), 0) >> 4) == iota((PACK, 16), 1))
    halves = []
    for part_of in split(evals[...]):
        halves.append(dot(jnp.where(keep, dot_last(basis_of, part_of), 0.0).astype(bf16), code_of))
    w_table[:, :16] = halves[0].astype(bf16)
    w_table[:, 16:] = halves[1].astype(bf16)


def find_links(devices, tiles, small, aux, from_top):
    me = lax.axis_index("dom").astype(f32)
    row = iota((ASKS, LANES), 0).astype(f32)
    up_to = one_hot(iota((LANES, LANES), 0) <= iota((LANES, LANES), 1))
    request = (iota((LANES, LANES), 0) & (REQ - 1)).astype(f32)
    carry = jnp.zeros((ASKS, 1), f32)
    wanted = jnp.zeros((2 * ASKS, LANES), f32)
    for tile in range(tiles):
        at = slice(tile * LANES, (tile + 1) * LANES)
        occupied = small[OCCUPIED : OCCUPIED + 1, at] > 0.5
        target = jnp.full((1, LANES), -1.0, f32)
        slots = jnp.zeros((1, LANES), f32)
        for face in range(4):
            link = small[LINK + face : LINK + face + 1, at]
            owner = jnp.floor((link + 0.5) * (1.0 / PARTITION_SLOTS))
            slot = link - owner * PARTITION_SLOTS
            near = owner == me
            aux[face : face + 1, at] = jnp.where(near, slot, -1.0).astype(i32)
            away = occupied & jnp.logical_not(near)
            target = jnp.where(away, owner, target)
            slots = jnp.where(away, slot, slots)
        far = target - me
        far = jnp.where(far < 0, far + devices, far)
        partner = jnp.where(far <= 4, far - 1.0, jnp.where(far >= devices - 4, devices + 3.0 - far, 8.0))
        partner = jnp.where(target >= 0, partner, -1.0)
        named = jnp.where(row == partner, 1.0, 0.0)
        prefix = dot(named.astype(bf16), up_to) + carry
        carry = carry + jnp.sum(named, axis=1, keepdims=True)
        rank = jnp.sum(named * prefix, axis=0, keepdims=True) - 1.0
        if from_top:
            rank = REQ - 1.0 - rank
        aux[4:5, at] = jnp.where(target >= 0, partner * REQ + rank, -1.0).astype(i32)
        aux[5:8, at] = jnp.zeros((3, LANES), i32)
        ask = slots + 1.0
        high = jnp.floor(ask * (1.0 / 32)) * 32.0
        both = jnp.concatenate([named * high, named * (ask - high)], axis=0).astype(bf16)
        wanted = wanted + dot_last(both, one_hot(request == rank))
    return wanted[:ASKS] + wanted[ASKS:]


def prepare_kernel(devices, tiles, normals, speed, cluster, slot, links, orient, q, jac, small, aux, asks, group, one, record):
    me = lax.axis_index("dom")
    for face in range(4):
        small[3 * face : 3 * face + 3, :] = jnp.concatenate([normals[d, face : face + 1, :] for d in range(3)], axis=0)
    small[SPEED : SPEED + 1, :] = speed[...]
    small[CLUSTER : CLUSTER + 1, :] = cluster[...].astype(f32)
    small[LINK : LINK + 4, :] = links[...].astype(f32)
    small[ORIENT : ORIENT + 4, :] = orient[...].astype(f32)
    where = slot[...]
    stays = (where >= me * PARTITION_SLOTS) & (where < (me + 1) * PARTITION_SLOTS)
    small[OCCUPIED : OCCUPIED + 1, :] = jnp.where(stays, 1.0, 0.0)
    small[OCCUPIED + 1 : SMALL, :] = jnp.zeros((1, tiles * LANES), f32)
    wanted = find_links(devices, tiles, small, aux, False)
    asks[...] = jnp.zeros((devices, 1, LANES), f32)
    for k, offset in enumerate(partner_offsets(devices)):
        asks[lax.rem(me + offset + devices, devices)] = wanted[k : k + 1]

    record[...] = jnp.zeros((RECORD, LANES), f32)
    for p in range(NV):
        record[p * NBP : p * NBP + NB] = q[p]
        for inner in range(NV):
            at = ROWS + 4 * (p * NV + inner)
            record[at : at + 3] = jac[p, inner]
    fields = small[:, KEEP:]
    row = iota(fields.shape, 0)
    record[JAC_END : JAC_END + SMALL] = jnp.where(row == OCCUPIED, 1.0 - fields, fields)
    whole = record[...]
    turned = jnp.concatenate([whole[c : c + LANES].T for c in range(0, RECORD, LANES)], axis=1)
    one[...] = turned[:CSZ]
    position = me // (devices // GROUPS)
    for g in range(GROUPS):
        group[lax.rem(position + g, GROUPS)] = turned[g * CSZ : (g + 1) * CSZ]


def prepare(normals, speed, cluster, slot, links, orient, q, jac, devices):
    count = q.shape[2]

    def body(*refs):
        prepare_kernel(devices, count // LANES, *refs)

    last = KEEP // LANES
    return pl.pallas_call(
        body,
        grid=(1,),
        in_specs=[
            whole_spec(normals),
            whole_spec(speed),
            whole_spec(cluster),
            whole_spec(slot),
            whole_spec(links),
            whole_spec(orient),
            pl.BlockSpec((NV, NB, LANES), lambda i: (0, 0, last)),
            pl.BlockSpec((NV, NV, 3, LANES), lambda i: (0, 0, 0, last)),
        ],
        out_specs=[
            pl.BlockSpec((SMALL, count), lambda i: (0, 0)),
            pl.BlockSpec((8, count), lambda i: (0, 0)),
            pl.BlockSpec((devices, 1, LANES), lambda i: (0, 0, 0)),
            pl.BlockSpec((GROUPS, CSZ, RECORD), lambda i: (0, 0, 0)),
            pl.BlockSpec((CSZ, RECORD), lambda i: (0, 0)),
        ],
        out_shape=[
            jax.ShapeDtypeStruct((SMALL, count), f32),
            jax.ShapeDtypeStruct((8, count), i32),
            jax.ShapeDtypeStruct((devices, 1, LANES), f32),
            jax.ShapeDtypeStruct((GROUPS, CSZ, RECORD), f32),
            jax.ShapeDtypeStruct((CSZ, RECORD), f32),
        ],
        scratch_shapes=[pltpu.VMEM((RECORD, LANES), f32)],
        compiler_params=MOST,
        name="prepare",
    )(normals, speed, cluster, slot, links, orient, q, jac)


def unpack(devices, group, one, q, jac, small, aux):
    position = lax.axis_index("dom") // (devices // GROUPS)
    rows = [one[...]]
    for g in range(1, GROUPS):
        rows.append(group[lax.rem(position - g + GROUPS, GROUPS)])
    whole = jnp.concatenate(rows, axis=0)
    turned = jnp.concatenate([whole[:, c : c + LANES].T for c in range(0, RECORD, LANES)], axis=0)
    for p in range(NV):
        q[p] = turned[p * NBP : p * NBP + NB]
        for inner in range(NV):
            at = ROWS + 4 * (p * NV + inner)
            jac[p, inner] = turned[at : at + 3]
    small[...] = turned[JAC_END : JAC_END + SMALL]
    return find_links(devices, 1, small, aux, True)


OUT_BLOCKS = {1: (0, 0), 4: (0, 1), -2: (0, 2), -1: (1, 0), -4: (1, 1), 2: (1, 2), 3: (2, 0), -3: (3, 0)}
IN_BLOCKS = {-1: (0, 0), 1: (1, 0), -3: (2, 0), -4: (2, 1), -2: (2, 2), 3: (3, 0), 4: (3, 1), 2: (3, 2)}


def put(outs, rows, k, devices):
    if k == PARTNERS - 1:
        return outs[4], 0
    array, block = OUT_BLOCKS[-partner_offsets(devices)[k]]
    return outs[array], block * rows


def take(messages, k, devices):
    if k == PARTNERS - 1:
        return messages[4], 0
    array, block = IN_BLOCKS[partner_offsets(devices)[k]]
    rows = messages[4].shape[0]
    return messages[array], block * rows


def picked(requests, fields):
    lane = iota((1, LANES), 1)
    tiles = []
    for at in range(0, 12, 4):
        four = [requests[min(at + n, PARTNERS - 1)] for n in range(4)]
        tiles.append(
            jnp.where(lane < 32, four[0], jnp.where(lane < 64, four[1], jnp.where(lane < 96, four[2], four[3])))
        )
    slots = (iota((KEEP, FAR), 0) + 1).astype(f32)
    return dot(fields, one_hot(slots == jnp.concatenate(tiles, axis=1)))


def message_rows(both):
    value = both[:PACK] + both[PACK:]
    return jnp.concatenate([value, jnp.zeros((MSG - PACK, FAR), f32)], axis=0).T


def back(k):
    return k if k == PARTNERS - 1 else (k + 4) % 8


def requests_here(devices, asks):
    me = lax.axis_index("dom")
    peers = [lax.rem(me - o + devices, devices) for o in partner_offsets(devices)]
    return [asks[p] for p in peers]


def unpack_kernel(devices, group, one, asks, field, q, jac, small, aux, *outs):
    moved = unpack(devices, group, one, q, jac, small, aux)
    rows = message_rows(picked(requests_here(devices, asks), field[...]))
    for k in range(PARTNERS):
        out, at = put(outs, MESSAGE1, k, devices)
        out[at : at + REQ] = rows[k * REQ : (k + 1) * REQ]
        out[at + REQ : at + MESSAGE1, :LANES] = jnp.broadcast_to(moved[back(k) : back(k) + 1, :], (8, LANES))
        out[at + REQ : at + MESSAGE1, LANES:] = jnp.zeros((8, MSG - LANES), f32)


def answer_again(devices, asks, got, field, later, outs):
    moved = []
    for k in range(PARTNERS):
        message, at = take(got, back(k), devices)
        moved.append(message[at + REQ : at + REQ + 1, :LANES])
    every = [a + b for a, b in zip(requests_here(devices, asks), moved)]
    rows = message_rows(picked(every, later))
    rows_first = message_rows(picked(moved, field))
    for k in range(PARTNERS):
        out, at = put(outs, 2 * REQ, k, devices)
        out[at : at + REQ] = rows[k * REQ : (k + 1) * REQ]
        out[at + REQ : at + 2 * REQ] = rows_first[k * REQ : (k + 1) * REQ]


def relay_kernel(got_plus, got_minus, own_plus, own_minus, on_plus, on_minus):
    rows = own_plus.shape[0]
    block = [slice(b * rows, (b + 1) * rows) for b in range(3)]
    on_plus[block[0]] = own_plus[...]
    on_plus[block[1]] = got_plus[block[1]]
    on_plus[block[2]] = got_minus[block[2]]
    on_minus[block[0]] = own_minus[...]
    on_minus[block[1]] = got_minus[block[1]]
    on_minus[block[2]] = got_plus[block[2]]


def message_shapes(rows):
    return [jax.ShapeDtypeStruct((rows * blocks, MSG), f32) for blocks in (3, 3, 1, 1, 1)]


def far_table(devices, part, messages):
    rows = []
    for k in range(PARTNERS):
        message, at = take(messages, k, devices)
        rows.append(message[at + part * REQ : at + (part + 1) * REQ, :])
    rows.append(jnp.zeros((FAR - PARTNERS * REQ, MSG), f32))
    turned = jnp.concatenate(rows, axis=0).T[:PACK]
    return jnp.concatenate(split(turned), axis=0)


def take_turns(*chains):
    results = [None] * len(chains)
    going = list(range(len(chains)))
    while going:
        for n in list(going):
            try:
                next(chains[n])
            except StopIteration as stop:
                results[n] = stop.value
                going.remove(n)
    return results


def alone(chain):
    return take_turns(chain)[0]


class Window:
    def __init__(self, ref, begin, width):
        self.ref, self.begin = ref, begin
        self.shape = tuple(ref.shape[:-1]) + (width,)

    def _at(self, index):
        rank = len(self.shape)
        if index is Ellipsis:
            index = ()
        index = index if isinstance(index, tuple) else (index,)
        index = index + (slice(None),) * (rank - len(index))
        low, high, _ = index[-1].indices(self.shape[-1])
        return index[:-1] + (slice(self.begin + low, self.begin + high),)

    def __getitem__(self, index):
        return self.ref[self._at(index)]

    def __setitem__(self, index, value):
        self.ref[self._at(index)] = value


def lanes(tile):
    return slice(tile * LANES, (tile + 1) * LANES)


def jacobian_apply(jac, tile, parts):
    result = [None] * NV
    for group in range(3):
        for d in range(3):
            for inner in range(3):
                q = 3 * group + inner
                value = parts(d, q)
                for p in range(NV):
                    term = jac[p, q, d : d + 1, lanes(tile)] * value
                    result[p] = term if result[p] is None else result[p] + term
    return result


def packed_split(fields, group):
    packed = [pack_three(tile[3 * group : 3 * group + 3]) for tile in fields]
    return split(jnp.concatenate(packed, axis=1))


def split_fields(fields):
    pairs = [packed_split(fields, group) for group in range(3)]
    return jnp.concatenate([a for a, _ in pairs] + [b for _, b in pairs], axis=0)


def predict(chains, w_pred):
    for state, _, sums in chains:
        for ref, scale in sums:
            for p in range(NV):
                ref[p] = scale[0] * state[p]

    def degree_step(degree, carry):
        turned = []
        for state, _, _ in chains:
            now = load_field(state)
            turned.append([dot(w_pred[...], stacked(*packed_split(now, group))) for group in range(3)])
        for (state, jac, sums), of in zip(chains, turned):
            scales = [jnp.where(degree == 1, s[1], jnp.where(degree == 2, s[2], s[3])) for _, s in sums]
            for t in range(state.shape[2] // LANES):
                at = lanes(t)
                result = jacobian_apply(
                    jac, t, lambda d, q: of[q // 3][d * 72 + (q % 3) * NBP : d * 72 + (q % 3) * NBP + NBP, at]
                )
                for p in range(NV):
                    state[p, :, at] = result[p]
                    for (ref, _), scale in zip(sums, scales):
                        ref[p, :, at] = ref[p, :, at] + scale * result[p]
        return carry

    lax.fori_loop(1, NORDER, degree_step, 0)


def face_products(gathered, table, tiles):
    outers = []
    for t in tiles:
        outer = [None] * NV
        for b in range(NB):
            values = table[b * NQ : (b + 1) * NQ, lanes(t)]
            for p in range(NV):
                at = packed_row(p, b)
                term = gathered[at : at + 1, lanes(t)] * values
                outer[p] = term if outer[p] is None else outer[p] + term
        outers.append(outer)
    return [
        stacked(*split(jnp.concatenate([jnp.concatenate(o[3 * g : 3 * g + 3], axis=0) for o in outers], axis=1)))
        for g in range(3)
    ]


def table_of(code, w_table):
    hot = one_hot(iota((16, code.shape[1]), 0).astype(f32) == code)
    return dot(w_table, jnp.concatenate([hot, hot], axis=0))


class NearChain:
    def __init__(self, near, weights, small, aux, gathered, table, by_face, parts):
        self.near, self.small, self.aux, self.gathered, self.table = near, small, aux, gathered, table
        self.by_face, self.parts = by_face, parts
        self.w_own, self.w_lift, self.w_table = weights
        self.count = aux.shape[-1]
        self.tiles = range(self.count // LANES)

    def begin(self, own):
        for group in range(3):
            rows = slice(64 * group, 64 * group + 64)
            lower = slice(PACK + 64 * group, PACK + 64 * group + 64)
            mine = dot(self.w_own[...], stacked(own[rows], own[lower]))
            for inner in range(3):
                q = 3 * group + inner
                of = [mine[72 * block + NBP * inner : 72 * block + NBP * inner + NBP] for block in range(8)]
                for d in range(3):
                    self.parts[d * NV + q] = of[d]
                for face in range(4):
                    self.by_face[face, q] = of[3 + face]
                self.parts[3 * NV + q] = of[7]

    def gather(self, face):
        count = self.count
        slots = iota((KEEP, count), 0).astype(jnp.int16)
        index = jnp.broadcast_to(self.aux[pl.ds(face, 1), :], (16, count)).astype(jnp.int16)
        index = jnp.concatenate([index] * (KEEP // 16), axis=0)
        both = dot(self.near[...], jnp.where(slots == index, jnp.ones((), bf16), jnp.zeros((), bf16)))
        self.gathered[...] = both[:PACK] + both[PACK:]
        self.table[...] = table_of(self.small[pl.ds(ORIENT + face, 1), :], self.w_table[...])

    def products(self, face):
        normals = [self.small[pl.ds(3 * face + d, 1), :] for d in range(3)]
        for group, points in enumerate(face_products(self.gathered, self.table, self.tiles)):
            lifted = dot(self.w_lift[face], points)
            for inner in range(3):
                q = 3 * group + inner
                at = inner * NBP
                mixed = lifted[at : at + NBP] + self.by_face[face, q]
                self.parts[3 * NV + q] = self.parts[3 * NV + q] + lifted[72 + at : 72 + at + NBP]
                for d in range(3):
                    self.parts[d * NV + q] = self.parts[d * NV + q] + normals[d] * mixed


def near_part(chains, owns):
    chains[0].gather(0)
    for chain, own in zip(chains, owns):
        chain.begin(own)

    def two_faces(pair, carry):
        for face in (2 * pair, 2 * pair + 1):
            for other in chains[1:]:
                other.gather(face)
            chains[0].products(face)
            chains[0].gather((face + 1) & 3)
            for other in chains[1:]:
                other.products(face)
        return carry

    lax.fori_loop(0, 2, two_faces, 0)


def update_chain(parts, far, small, aux, jac, w_far, w_table, gathered):
    volume, upwind = parts
    tiles = range(len(volume))
    count = len(volume) * LANES
    place = aux[4:5, :]
    both = dot(far, one_hot(iota((FAR, count), 0) == place))
    gathered[...] = both[:PACK] + both[PACK:]
    masks = [jnp.where((aux[face : face + 1, :] < 0) & (place >= 0), 1.0, 0.0) for face in range(4)]
    code = masks[0] * small[ORIENT : ORIENT + 1, :]
    normals = [masks[0] * small[d : d + 1, :] for d in range(3)]
    for face in range(1, 4):
        code = code + masks[face] * small[ORIENT + face : ORIENT + face + 1, :]
        normals = [n + masks[face] * small[3 * face + d : 3 * face + d + 1, :] for d, n in enumerate(normals)]
    changes = [[None] * NV for t in tiles]
    table = table_of(code, w_table)
    yield
    volume = [[list(v) for v in tile] for tile in volume]
    upwind = [list(tile) for tile in upwind]
    for group, points in enumerate(face_products(gathered, table, tiles)):
        lifted = dot(w_far, points)
        for t in tiles:
            for inner in range(3):
                q = 3 * group + inner
                mixed = None
                for face in range(4):
                    at = 72 * face + inner * NBP
                    term = masks[face][:, lanes(t)] * lifted[at : at + NBP, lanes(t)]
                    mixed = term if mixed is None else mixed + term
                upwind[t][q] = upwind[t][q] - mixed
                for d in range(3):
                    volume[t][d][q] = volume[t][d][q] + normals[d][:, lanes(t)] * mixed
    for t in tiles:
        change = jacobian_apply(jac, t, lambda d, q: volume[t][d][q])
        speed = small[SPEED : SPEED + 1, lanes(t)]
        changes[t] = [c + speed * u for c, u in zip(change, upwind[t])]
    return changes


def update(*args):
    return alone(update_chain(*args))


def load_parts(ref):
    tiles = range(ref.shape[2] // LANES)
    volume = [[[ref[d * NV + q, :, lanes(t)] for q in range(NV)] for d in range(3)] for t in tiles]
    return volume, [[ref[3 * NV + q, :, lanes(t)] for q in range(NV)] for t in tiles]


def load_state(q, padded):
    padded[:, NB:NBP, :] = jnp.zeros((NV, NBP - NB, padded.shape[2]), f32)
    for p in range(NV):
        padded[p, :NB, :] = q[p]
    return load_field(padded)


def load_field(ref):
    return [[ref[p, :, lanes(t)] for p in range(NV)] for t in range(ref.shape[2] // LANES)]


def store_field(ref, field):
    for t, tile in enumerate(field):
        for p in range(NV):
            ref[p, :, lanes(t)] = tile[p]


def store_result(out, base, change, small):
    for t in range(len(base)):
        occupied = small[OCCUPIED : OCCUPIED + 1, lanes(t)] > 0.5
        for p in range(NV):
            out[p, :, lanes(t)] = jnp.where(occupied, base[t][p] + change[t][p], 0.0)[:NB]


def first_kernel(
    q, jac, deriv, stiff, evals, lift, packed, slow, w_pred, w_own, w_lift, w_table, w_far, padded, sums, square
):
    @pl.when(pl.program_id(0) == 0)
    def _():
        make_weights(deriv, stiff, evals, lift, w_pred, w_own, w_lift, w_table, w_far, square)

    load_state(q, padded)
    chains = []
    for begin in range(0, BOTH, WIDE):
        state, jacobians, early, late = [Window(r, begin, WIDE) for r in (padded, jac, sums, slow)]
        chains.append((state, jacobians, [(early, FIRST), (late, SECOND)]))
    predict(chains, w_pred)
    packed[...] = split_fields(load_field(sums))


def near_kernel(own, near, small, aux, w_own, w_lift, w_table, *refs):
    parts, gathered, table, by_face = refs[-4:]
    chains, owns = [], []
    for begin in range(0, BOTH, WIDE):
        windows = [Window(r, begin, WIDE) for r in (small, aux, gathered, table, by_face, parts)]
        chains.append(NearChain(near, (w_own, w_lift, w_table), *windows))
        owns.append(Window(own, begin, WIDE))
    near_part(chains, owns)


def middle_steps(chains, far, w_pred, w_far, w_table):
    updates = []
    for _, parts, jac, small, _, aux, gathered, _, _, _ in chains:
        updates.append(update_chain(load_parts(parts), far, small, aux, jac, w_far, w_table, gathered))
    for chain, change in zip(chains, take_turns(*updates)):
        q, _, _, small, _, _, _, base, state, _ = chain
        start = load_state(q, state)
        for t in range(len(start)):
            fast = small[CLUSTER : CLUSTER + 1, lanes(t)] < 0.5
            for p in range(NV):
                now = start[t][p] + change[t][p]
                base[p, :, lanes(t)] = now
                state[p, :, lanes(t)] = jnp.where(fast, now, start[t][p])
    predict([(chain[8], chain[2], [(chain[9], FIRST)]) for chain in chains], w_pred)
    results = []
    for _, _, _, small, slow, _, _, _, _, sums in chains:
        second = []
        for t, (late, later) in enumerate(zip(load_field(slow), load_field(sums))):
            fast = small[CLUSTER : CLUSTER + 1, lanes(t)] < 0.5
            second.append([jnp.where(fast, a, b) for a, b in zip(later, late)])
        results.append(split_fields(second))
    return results


def middle_kernel(devices, steps, q, jac, small, slow, parts, near, aux, asks, *refs):
    messages = refs[:5]
    w_pred, w_far, w_table, base, packed, *outs, padded, sums, gathered, far = refs[5:]
    step = pl.program_id(0)

    @pl.when(step == 0)
    def _():
        far[...] = far_table(devices, 0, messages)

    refs = (q, parts, jac, small, slow, aux, gathered, base, padded, sums)
    chains = [[Window(r, begin, WIDE) for r in refs] for begin in range(0, BOTH, WIDE)]
    second = jnp.concatenate(middle_steps(chains, far[...], w_pred, w_far[...], w_table[...]), axis=1)
    packed[:, pl.ds(pl.multiple_of(step * BOTH, BOTH), BOTH)] = second

    @pl.when(step == steps - 1)
    def _():
        answer_again(devices, asks, messages, near[...], packed[:, :KEEP], outs)


def last_kernel(
    devices, steps, base, jac, small, parts, aux, q_moved, jac_moved, small_moved, aux_moved, near, later, *refs
):
    messages = refs[:5]
    w_pred, w_own, w_lift, w_table, w_far, out, gathered, far = refs[5:13]
    padded, gathered_moved, table, by_face, parts_moved, early, late, now = refs[13:]
    step = pl.program_id(0)

    @pl.when(step == 0)
    def _():
        far[...] = far_table(devices, 0, messages)

    @pl.when(step < steps)
    def _():
        table_far = far[...]
        chains, stores = [], []
        for begin in range(0, BOTH, WIDE):
            w = [Window(r, begin, WIDE) for r in (parts, small, aux, jac, gathered, out, base)]
            chains.append(
                update_chain(load_parts(w[0]), table_far, w[1], w[2], w[3], w_far[...], w_table[...], w[4])
            )
            stores.append((w[5], w[6], w[1]))
        for (to, start, fields), change in zip(stores, take_turns(*chains)):
            store_result(to, load_field(start), change, fields)

    @pl.when(step == steps)
    def _():
        load_state(q_moved, padded)
        predict([(padded, jac_moved, [(early, FIRST), (late, SECOND)])], w_pred)
        chain = NearChain(
            near, (w_own, w_lift, w_table), small_moved, aux_moved, gathered_moved, table, by_face, parts_moved
        )
        near_part([chain], [split_fields(load_field(early))])
        fields = (q_moved, parts_moved, jac_moved, small_moved, late, aux_moved, gathered_moved, now, padded, early)
        far_first = far_table(devices, 1, messages)
        (second,) = middle_steps([fields], far_first, w_pred, w_far[...], w_table[...])
        chain.near = later
        near_part([chain], [second])
        change = update(
            load_parts(parts_moved), far[...], small_moved, aux_moved, jac_moved, w_far[...], w_table[...],
            gathered_moved,
        )
        store_result(out, load_field(now), change, small_moved)


def whole_spec(array):
    rank = array.ndim
    return pl.BlockSpec(array.shape, lambda i: (0,) * rank)


def lane_spec(*lead, last=None):
    rank = len(lead)
    if last is None:
        return pl.BlockSpec(lead + (WIDE,), lambda i: (0,) * rank + (i,))
    return pl.BlockSpec(lead + (BOTH,), lambda i: (0,) * rank + (jnp.minimum(i, last),))


Q_SPEC = lane_spec(NV, NB)
J_SPEC = lane_spec(NV, NV, 3)
S_SPEC = lane_spec(SMALL)
A_SPEC = lane_spec(8)
F_SPEC = lane_spec(NV, NBP)
X_SPEC = lane_spec(2 * PACK)
N_SPEC = pl.BlockSpec((2 * PACK, KEEP), lambda i: (0, 0))


def padded_scratch(width):
    return pltpu.VMEM((NV, NBP, width), f32)


def gathered_scratch(width):
    return pltpu.VMEM((PACK, width), f32)


def near_scratch(width):
    return [gathered_scratch(width), pltpu.VMEM((320, width), f32), pltpu.VMEM((4, NV, NBP, width), f32)]


def per_device(
    element_freedom_values,
    scaled_jacobian_matrices,
    outward_face_normals,
    largest_wave_speed,
    element_cluster_index,
    element_new_slot,
    neighbours,
    face_rotation_codes,
    deriv_mats,
    stiff_mats,
    face_eval,
    face_lift,
):
    count = element_freedom_values.shape[2]
    steps = count // WIDE
    devices = lax.axis_size("dom")
    q = element_freedom_values
    jac = jnp.transpose(scaled_jacobian_matrices, (1, 2, 0, 3))

    def shift(array, by):
        return lax.ppermute(array, "dom", [(i, (i + by) % devices) for i in range(devices)])

    def swap(array, groups):
        return lax.all_to_all(array, "dom", split_axis=0, concat_axis=0, axis_index_groups=groups, tiled=True)

    def on_ring(body):
        def kernel(*refs):
            body(devices, *refs)

        return kernel

    small, aux, asks, group, one = prepare(
        jnp.transpose(outward_face_normals, (1, 0, 2)),
        largest_wave_speed[None],
        element_cluster_index[None],
        element_new_slot[None],
        neighbours,
        face_rotation_codes,
        q,
        jac,
        devices,
    )
    asks = swap(asks, None)
    asks, group, one = lax.optimization_barrier((asks, group, one))
    stride = devices // GROUPS
    group = swap(group, [[r + stride * j for j in range(GROUPS)] for r in range(stride)])
    one = shift(one, 1)
    packed_shape = jax.ShapeDtypeStruct((2 * PACK, count), bf16)
    field_shape = jax.ShapeDtypeStruct((NV, NBP, count), f32)
    far = pltpu.VMEM((2 * PACK, FAR), bf16)
    weight_shapes = [
        jax.ShapeDtypeStruct((ROWS, PACK), bf16),
        jax.ShapeDtypeStruct((576, PACK), bf16),
        jax.ShapeDtypeStruct((4, 144, 144), bf16),
        jax.ShapeDtypeStruct((320, 32), bf16),
        jax.ShapeDtypeStruct((288, 144), bf16),
    ]
    evals = jnp.transpose(face_eval, (0, 2, 1)).reshape(12 * NQ, NB)
    matrices = [deriv_mats, stiff_mats, evals, face_lift]
    halves = count // BOTH

    def part_spec(begin, *lead):
        rank = len(lead)
        return pl.BlockSpec(lead + (BOTH,), lambda i: (0,) * rank + (i + begin,))

    first, slow, w_pred, w_own, w_lift, w_table, w_far = pl.pallas_call(
        first_kernel,
        grid=(halves,),
        in_specs=[part_spec(0, NV, NB), part_spec(0, NV, NV, 3)] + [whole_spec(m) for m in matrices],
        out_specs=[part_spec(0, 2 * PACK), part_spec(0, NV, NBP)] + [whole_spec(w) for w in weight_shapes],
        out_shape=[packed_shape, field_shape] + weight_shapes,
        scratch_shapes=[padded_scratch(BOTH), padded_scratch(BOTH), pltpu.VMEM((LANES, LANES), f32)],
        compiler_params=MOST,
        name="first",
    )(q, jac, *matrices)

    moved_shapes = [
        jax.ShapeDtypeStruct((NV, NB, LANES), f32),
        jax.ShapeDtypeStruct((NV, NV, 3, LANES), f32),
        jax.ShapeDtypeStruct((SMALL, LANES), f32),
        jax.ShapeDtypeStruct((8, LANES), i32),
    ]
    out_shape = moved_shapes + message_shapes(MESSAGE1)
    *moved, m0, m1, m2, m3, m4 = pl.pallas_call(
        on_ring(unpack_kernel),
        grid=(1,),
        in_specs=[whole_spec(a) for a in (group, one, asks)] + [N_SPEC],
        out_specs=[whole_spec(o) for o in out_shape],
        out_shape=out_shape,
        compiler_params=MOST,
        name="unpack",
    )(group, one, asks, first)
    of_near = [w_own, w_lift, w_table]
    parts_shape = jax.ShapeDtypeStruct((4 * NV, NBP, count), f32)

    def near_steps(field, begin, number, parts):
        def spec(*lead):
            return part_spec(begin, *lead)

        return pl.pallas_call(
            near_kernel,
            grid=(number,),
            in_specs=[spec(2 * PACK), N_SPEC, spec(SMALL), spec(8)]
            + [whole_spec(w) for w in of_near]
            + [pl.BlockSpec(memory_space=pl.ANY)] * len(parts),
            out_specs=spec(4 * NV, NBP),
            out_shape=parts_shape,
            scratch_shapes=near_scratch(BOTH),
            input_output_aliases={7: 0} if parts else {},
            cost_estimate=pl.CostEstimate(flops=int(4e9) * number, bytes_accessed=4 << 20, transcendentals=0),
            compiler_params=PARAMS,
            name="near",
        )(field, field, small, aux, *of_near, *parts)

    def exchange_beside(answers, field):
        half = halves // 2
        plus, minus, own_plus, own_minus, opposite = answers
        got_plus, got_minus, opposite = shift(plus, 1), shift(minus, -1), shift(opposite, devices // 2)
        parts = near_steps(field, 0, half, [])
        got_plus, got_minus, opposite, parts = lax.optimization_barrier((got_plus, got_minus, opposite, parts))
        on_plus, on_minus = pl.pallas_call(
            relay_kernel,
            out_shape=[jax.ShapeDtypeStruct(plus.shape, f32)] * 2,
            compiler_params=pltpu.CompilerParams(vmem_limit_bytes=4 << 20),
            name="relay",
        )(got_plus, got_minus, own_plus, own_minus)
        on_plus, on_minus = shift(on_plus, 3), shift(on_minus, -3)
        parts = near_steps(field, half, halves - half, [parts])
        return (got_plus, got_minus, on_plus, on_minus, opposite), parts

    messages, parts = exchange_beside((m0, m1, m2, m3, m4), first)

    def middle(*refs):
        middle_kernel(devices, halves, *refs)

    weights = [w_pred, w_far, w_table]
    out_shape = [field_shape, packed_shape] + message_shapes(2 * REQ)
    base, second, *answers = pl.pallas_call(
        middle,
        grid=(halves,),
        in_specs=[
            part_spec(0, NV, NB),
            part_spec(0, NV, NV, 3),
            part_spec(0, SMALL),
            part_spec(0, NV, NBP),
            part_spec(0, 4 * NV, NBP),
            N_SPEC,
            part_spec(0, 8),
            whole_spec(asks),
        ]
        + [whole_spec(a) for a in (*messages, *weights)],
        out_specs=[part_spec(0, NV, NBP)] + [whole_spec(o) for o in out_shape[1:]],
        out_shape=out_shape,
        scratch_shapes=[padded_scratch(BOTH), padded_scratch(BOTH), gathered_scratch(BOTH), far],
        compiler_params=PARAMS,
        name="middle",
    )(q, jac, small, slow, parts, first, aux, asks, *messages, *weights)
    messages, parts = exchange_beside(answers, second)

    def last(*refs):
        last_kernel(devices, halves, *refs)

    end = halves - 1
    weights = [w_pred, w_own, w_lift, w_table, w_far]
    return pl.pallas_call(
        last,
        grid=(halves + 1,),
        in_specs=[
            lane_spec(NV, NBP, last=end),
            lane_spec(NV, NV, 3, last=end),
            lane_spec(SMALL, last=end),
            lane_spec(4 * NV, NBP, last=end),
            lane_spec(8, last=end),
        ]
        + [whole_spec(a) for a in moved]
        + [N_SPEC, N_SPEC]
        + [whole_spec(a) for a in (*messages, *weights)],
        out_specs=part_spec(0, NV, NB),
        out_shape=jax.ShapeDtypeStruct((NV, NB, PARTITION_SLOTS), f32),
        scratch_shapes=[
            gathered_scratch(BOTH),
            far,
            padded_scratch(LANES),
            *near_scratch(LANES),
            pltpu.VMEM((4 * NV, NBP, LANES), f32),
            *[padded_scratch(LANES)] * 3,
        ],
        compiler_params=PARAMS,
        name="last",
    )(base, jac, small, parts, aux, *moved, first, second, *messages, *weights)


def solution(mesh):
    placed = (
        P(None, None, "dom"),
        P(None, None, None, "dom"),
        P(None, None, "dom"),
        P("dom"),
        P("dom"),
        P("dom"),
        P(None, "dom"),
        P(None, "dom"),
        P(),
        P(),
        P(),
        P(),
    )
    return jax.shard_map(
        per_device, mesh=mesh, in_specs=placed, out_specs=P(None, None, "dom"), check_vma=False
    )
```

profile of v0, /device:TPU:0, one launch (start us, length us, event | category | flops | bytes accessed | tf_op | source)
XLA Modules:
  0.0 114.3 jit_solution(451939474690421122)
XLA Ops:
  0.0 2.5 %prepare.1 = (f32[24,1024]{1,0:T(8,128)}, s32[8,1024]{1,0:T(8,128)}, f32[32,1,128]{2,1,0:T(1,128)}, f32[8,16,640]{2,1,0:T(8,128)}, f32[16,640]{1,0:T(8,128)}) custom-call(f32[3,4,1024]{2,1,0:T(4,128)} %bitcast.13, f32[1,1024]{1,0:T(1,128)} %bitcast.14, s32[1,1024]{1,0:T(1,128)} %bitcast.15, s32[1,1024]{1,0:T(1,128)} %bitcast.16, s32[4,1024]{1,0:T(4,128)} %refs_4_.1, ...), custom_call_target="tpu_custom_call" | custom-call | tf_op jit(solution)/shard_map/prepare/pallas_call | solution.py:242
  2.5 14.5 %all_to_all.10.refs_2_.refs_7_ = f32[32,1,128]{2,1,0:T(1,128)} all-to-all(f32[32,1,128]{2,1,0:T(1,128)} %get-tuple-element.55), channel_id=1, replica_groups=mesh['dom'=32] {'dom'}, dimensions={0} | all-to-all | bytes 32768 | tf_op jit(solution)/shard_map/all_to_all | solution.py:805
  17.0 3.4 %all-to-all-start.1 = ((f32[8,16,640]{2,1,0:T(8,128)}), f32[8,16,640]{2,1,0:T(8,128)S(1)}, u32[]{:S(2)}, u32[]{:S(2)}) async-start(f32[8,16,640]{2,1,0:T(8,128)} %get-tuple-element.58), calls=%async_computation.1 | async-start | bytes 655360 | tf_op jit(solution)/shard_map/all_to_all | solution.py:805
  20.5 0.1 collective-permute-start
  20.5 11.7 %first.1 = (bf16[384,1024]{1,0:T(8,128)(2,1)}, f32[9,24,1024]{2,1,0:T(8,128)}, bf16[216,192]{1,0:T(8,128)(2,1)}, bf16[576,192]{1,0:T(8,128)(2,1)}, bf16[4,144,14...) custom-call(f32[9,20,1024]{2,1,0:T(8,128)} %refs_0_.1, f32[9,9,3,1024]{3,2,1,0:T(4,128)} %bitcast.9, ...), custom_call_target="tpu_custom_call" | custom-call | tf_op jit(solution)/shard_map/first/pallas_call | solution.py:847
  32.3 0.0 all-to-all-done.1.refs_0_
  32.3 0.6 copy-done.21
  32.9 0.1 copy-done.20
  33.0 2.9 %unpack.1 = (f32[9,20,128]{2,1,0:T(8,128)}, f32[9,9,3,128]{3,2,1,0:T(4,128)}, f32[24,128]{1,0:T(8,128)}, s32[8,128]{1,0:T(8,128)}, f32[120,256]{1,0:T(8,128)}, /...) custom-call(f32[8,16,640]{2,1,0:T(8,128)} %copy-done.20, f32[16,640]{1,0:T(8,128)} %copy-done.21, ...), custom_call_target="tpu_custom_call" | custom-call | tf_op jit(solution)/shard_map/unpack/pallas_call | solution.py:865
  35.9 2.8 %collective-permute-start.3 = (f32[40,256]{1,0:T(8,128)}, f32[40,256]{1,0:T(8,128)S(1)}, u32[]{:S(2)}, u32[]{:S(2)}) collective-permute-start(f32[40,256]{1,0:T(8,128)} %get-tuple-element.63), channel_id=1, source_target_pairs={{0,16},{1,17},{2,18},{3,19},{4,20},{5,21},{6,22},{7,23},{8,24},{9,... | collective-permute-start | bytes 122888 | tf_op jit(solution)/shard_map/ppermute | solution.py:802
  38.7 0.3 collective-permute-start.1
  39.0 5.0 %collective-permute-start.2 = (f32[120,256]{1,0:T(8,128)}, f32[120,256]{1,0:T(8,128)S(1)}, u32[]{:S(2)}, u32[]{:S(2)}) collective-permute-start(f32[120,256]{1,0:T(8,128)} %get-tuple-element.62), channel_id=1, source_target_pairs={{0,31},{1,0},{2,1},{3,2},{4,3},{5,4},{6,5},{7,6},{8,7},{9,8},{10,9... | collective-permute-start | bytes 368648 | tf_op jit(solution)/shard_map/ppermute | solution.py:802
  44.0 1.1 copy-done.2
  45.2 0.9 copy-done.8
  46.0 1.0 copy-done.9
  47.0 1.0 copy-done.10
  48.0 5.1 %near.4.refs_0_ = f32[36,24,1024]{2,1,0:T(8,128)S(1)} custom-call(bf16[384,1024]{1,0:T(8,128)(2,1)S(1)} %copy-done.2, bf16[384,1024]{1,0:T(8,128)(2,1)S(1)} %copy-done.2, f32[24,1024]{1,0:T(8,128)S(1)} %copy-done.7, s32[8,1024]{1,0:T(8,128)S(1)} %copy-done.14, bf16[576,192]{1,0:T(8,128)(2,1)S(1)} %copy-done.9, bf16[4,144,144]{2,1,0:T(8,128)(2,1)S(1)} %copy-done.10, ...), custom_call_target="tpu_custom_call" | custom-call | flops 4000000000 | bytes 4194304 | tf_op jit(solution)/shard_map/near/pallas_call | solution.py:881
  53.2 0.1 collective-permute-start.4
  53.2 0.0 copy-start
  53.3 0.0 copy-start.1
  53.3 0.0 copy-start.4
  53.3 4.6 %collective-permute-start.5 = (f32[120,256]{1,0:T(8,128)S(1)}, f32[120,256]{1,0:T(8,128)S(1)}, u32[]{:S(2)}, u32[]{:S(2)}) collective-permute-start(f32[120,256]{1,0:T(8,128)S(1)} %get-tuple-element.70), channel_id=1, source_target_pairs={{0,29},{1,30},{2,31},{3,0},{4,1},{5,2},{6,3},{7,4},{8,5},{9,6},{10... | collective-permute-start | bytes 368648 | tf_op jit(solution)/shard_map/ppermute | solution.py:802
  57.9 5.1 %near.5.refs_4_ = f32[36,24,1024]{2,1,0:T(8,128)S(1)} custom-call(bf16[384,1024]{1,0:T(8,128)(2,1)S(1)} %copy-done.2, bf16[384,1024]{1,0:T(8,128)(2,1)S(1)} %copy-done.2, f32[24,1024]{1,0:T(8,128)S(1)} %copy-done.7, s32[8,1024]{1,0:T(8,128)S(1)} %copy-done.14, bf16[576,192]{1,0:T(8,128)(2,1)S(1)} %copy-done.9, ...), custom_call_target="tpu_custom_call", output_to_operand_aliasing={{}: (7, {})} | custom-call | flops 4000000000 | bytes 4194304 | tf_op jit(solution)/shard_map/near/pallas_call | solution.py:881
  63.2 14.5 %middle.1 = (f32[9,24,1024]{2,1,0:T(8,128)S(1)}, bf16[384,1024]{1,0:T(8,128)(2,1)S(1)}, f32[192,256]{1,0:T(8,128)S(1)}, f32[192,256]{1,0:T(8,128)S(1)}, f32[64,2...) custom-call(f32[9,20,1024]{2,1,0:T(8,128)S(1)} %copy-done.1, f32[9,9,3,1024]{3,2,1,0:T(4,128)S(1)} %bitcast.10, ...), custom_call_target="tpu_custom_call" | custom-call | tf_op jit(solution)/shard_map/middle/pallas_call | solution.py:919
  77.7 0.1 collective-permute-start.8
  77.7 0.1 collective-permute-start.6
  77.8 5.3 %collective-permute-start.7 = (f32[192,256]{1,0:T(8,128)S(1)}, f32[192,256]{1,0:T(8,128)S(1)}, u32[]{:S(2)}, u32[]{:S(2)}) collective-permute-start(f32[192,256]{1,0:T(8,128)S(1)} %get-tuple-element.77), channel_id=1, source_target_pairs={{0,31},{1,0},{2,1},{3,2},{4,3},{5,4},{6,5},{7,6},{8,7},{9,8},{10,9... | collective-permute-start | bytes 589832 | tf_op jit(solution)/shard_map/ppermute | solution.py:802
  83.1 5.1 %near.6.refs_0_ = f32[36,24,1024]{2,1,0:T(8,128)S(1)} custom-call(bf16[384,1024]{1,0:T(8,128)(2,1)S(1)} %get-tuple-element.75.own.near.refs_10_, bf16[384,1024]{1,0:T(8,128)(2,1)S(1)} %get-tuple-element.75.own.near.refs_10_, f32[24,1024]{1,0:T(8,128)S(1)} %copy-done.7, s32[8,1024]{1,0:T(8,128)S(1)} %copy-done.14, bf16[576,192]{1,0:T(8,128)(2,1)S(1)} %copy-done.9, ...), custom_call_target="tpu_custom_call" | custom-call | flops 4000000000 | bytes 4194304 | tf_op jit(solution)/shard_map/near/pallas_call | solution.py:881
  88.3 0.1 collective-permute-start.9
  88.5 4.7 %collective-permute-start.10 = (f32[192,256]{1,0:T(8,128)S(1)}, f32[192,256]{1,0:T(8,128)S(1)}, u32[]{:S(2)}, u32[]{:S(2)}) collective-permute-start(f32[192,256]{1,0:T(8,128)S(1)} %get-tuple-element.89), channel_id=1, source_target_pairs={{0,29},{1,30},{2,31},{3,0},{4,1},{5,2},{6,3},{7,4},{8,5},{9,6},{10... | collective-permute-start | bytes 589832 | tf_op jit(solution)/shard_map/ppermute | solution.py:802
  93.1 5.1 %near.7.refs_3_ = f32[36,24,1024]{2,1,0:T(8,128)S(1)} custom-call(bf16[384,1024]{1,0:T(8,128)(2,1)S(1)} %get-tuple-element.75.own.near.refs_10_, bf16[384,1024]{1,0:T(8,128)(2,1)S(1)} %get-tuple-element.75.own.near.refs_10_, f32[24,1024]{1,0:T(8,128)S(1)} %copy-done.7, s32[8,1024]{1,0:T(8,128)S(1)} %copy-done.14, ...), custom_call_target="tpu_custom_call", output_to_operand_aliasing={{}: (7, {})} | custom-call | flops 4000000000 | bytes 4194304 | tf_op jit(solution)/shard_map/near/pallas_call | solution.py:881
  98.4 16.0 %last.1 = f32[9,20,1152]{2,1,0:T(8,128)} custom-call(f32[9,24,1024]{2,1,0:T(8,128)S(1)} %get-tuple-element.74.refs_0_, f32[9,9,3,1024]{3,2,1,0:T(4,128)S(1)} %bitcast.11, f32[24,1024]{1,0:T(8,128)S(1)} %copy-done.7, f32[36,24,1024]{2,1,0:T(8,128)S(1)} %near.7.refs_3_, s32[8,1024]{1,0:T(8,128)S(1)} %copy-done.14, f32[9,20,128]{2,1,0:T(8,128)S(1)} %copy-done.15, ...), custom_call_target="tpu_custom_call" | custom-call | tf_op jit(solution)/shard_map/last/pallas_call | solution.py:946
  (48 shorter events, 0.1 us)
Async XLA Ops:
  2.5 41.5 %copy-start.7 = (f32[24,1024]{1,0:T(8,128)S(1)}, f32[24,1024]{1,0:T(8,128)}, u32[]{:S(2)}) copy-start(f32[24,1024]{1,0:T(8,128)} %get-tuple-element.48.small.refs_2_) | copy-start | bytes 294916
  2.5 41.5 %copy-start.14 = (s32[8,1024]{1,0:T(8,128)S(1)}, s32[8,1024]{1,0:T(8,128)}, u32[]{:S(2)}) copy-start(s32[8,1024]{1,0:T(8,128)} %get-tuple-element.51.aux.refs_6_.refs_4_) | copy-start | bytes 98308
  17.0 15.3 %all-to-all-start.1 = ((f32[8,16,640]{2,1,0:T(8,128)}), f32[8,16,640]{2,1,0:T(8,128)S(1)}, u32[]{:S(2)}, u32[]{:S(2)}) async-start(f32[8,16,640]{2,1,0:T(8,128)} %get-tuple-element.58), calls=%async_computation.1 | async-start | bytes 655360 | tf_op jit(solution)/shard_map/all_to_all | solution.py:805
  20.5 11.8 %collective-permute-start = (f32[16,640]{1,0:T(8,128)}, f32[16,640]{1,0:T(8,128)S(1)}, u32[]{:S(2)}, u32[]{:S(2)}) collective-permute-start(f32[16,640]{1,0:T(8,128)} %get-tuple-element.59), channel_id=1, source_target_pairs={{0,1},{1,2},{2,3},{3,4},{4,5},{5,6},{6,7},{7,8},{8,9},{9,10},{10,1... | collective-permute-start | bytes 122888 | tf_op jit(solution)/shard_map/ppermute | solution.py:802
  35.9 17.2 %collective-permute-start.3 = (f32[40,256]{1,0:T(8,128)}, f32[40,256]{1,0:T(8,128)S(1)}, u32[]{:S(2)}, u32[]{:S(2)}) collective-permute-start(f32[40,256]{1,0:T(8,128)} %get-tuple-element.63), channel_id=1, source_target_pairs={{0,16},{1,17},{2,18},{3,19},{4,20},{5,21},{6,22},{7,23},{8,24},{9,... | collective-permute-start | bytes 122888 | tf_op jit(solution)/shard_map/ppermute | solution.py:802
  38.7 14.5 %collective-permute-start.1 = (f32[120,256]{1,0:T(8,128)}, f32[120,256]{1,0:T(8,128)S(1)}, u32[]{:S(2)}, u32[]{:S(2)}) collective-permute-start(f32[120,256]{1,0:T(8,128)} %get-tuple-element.61), channel_id=1, source_target_pairs={{0,1},{1,2},{2,3},{3,4},{4,5},{5,6},{6,7},{7,8},{8,9},{9,10},{10,1... | collective-permute-start | bytes 368648 | tf_op jit(solution)/shard_map/ppermute | solution.py:802
  39.0 14.1 %collective-permute-start.2 = (f32[120,256]{1,0:T(8,128)}, f32[120,256]{1,0:T(8,128)S(1)}, u32[]{:S(2)}, u32[]{:S(2)}) collective-permute-start(f32[120,256]{1,0:T(8,128)} %get-tuple-element.62), channel_id=1, source_target_pairs={{0,31},{1,0},{2,1},{3,2},{4,3},{5,4},{6,5},{7,6},{8,7},{9,8},{10,9... | collective-permute-start | bytes 368648 | tf_op jit(solution)/shard_map/ppermute | solution.py:802
  44.0 1.1 copy-start.2
  45.1 0.9 copy-start.8
  46.0 1.0 copy-start.9
  47.0 1.0 copy-start.10
  48.0 5.2 %copy-start.16 = (f32[40,256]{1,0:T(8,128)S(1)}, f32[40,256]{1,0:T(8,128)}, u32[]{:S(2)}) copy-start(f32[40,256]{1,0:T(8,128)} %get-tuple-element.67.own_plus) | copy-start | bytes 122884
  48.0 5.2 %copy-start.17 = (f32[40,256]{1,0:T(8,128)S(1)}, f32[40,256]{1,0:T(8,128)}, u32[]{:S(2)}) copy-start(f32[40,256]{1,0:T(8,128)} %get-tuple-element.68.own_minus) | copy-start | bytes 122884
  53.2 9.9 %collective-permute-start.4 = (f32[120,256]{1,0:T(8,128)S(1)}, f32[120,256]{1,0:T(8,128)S(1)}, u32[]{:S(2)}, u32[]{:S(2)}) collective-permute-start(f32[120,256]{1,0:T(8,128)S(1)} %get-tuple-element.69), channel_id=1, source_target_pairs={{0,3},{1,4},{2,5},{3,6},{4,7},{5,8},{6,9},{7,10},{8,11},{9,12},{10... | collective-permute-start | bytes 368648 | tf_op jit(solution)/shard_map/ppermute | solution.py:802
  53.2 9.8 %copy-start = (f32[3,9,9,1024]{3,0,2,1:T(4,128)S(1)}, f32[3,9,9,1024]{3,0,2,1:T(4,128)}, u32[]{:S(2)}) copy-start(f32[3,9,9,1024]{3,0,2,1:T(4,128)} %param.13) | copy-start | bytes 2985988
  53.3 9.8 %copy-start.1 = (f32[9,20,1024]{2,1,0:T(8,128)S(1)}, f32[9,20,1024]{2,1,0:T(8,128)}, u32[]{:S(2)}) copy-start(f32[9,20,1024]{2,1,0:T(8,128)} %refs_0_.1) | copy-start | bytes 2211844
  53.3 9.8 %copy-start.4 = (f32[9,24,1024]{2,1,0:T(8,128)S(1)}, f32[9,24,1024]{2,1,0:T(8,128)}, u32[]{:S(2)}) copy-start(f32[9,24,1024]{2,1,0:T(8,128)} %get-tuple-element.49.refs_3_) | copy-start | bytes 2654212
  53.3 9.8 %copy-start.5 = (bf16[288,144]{1,0:T(8,128)(2,1)S(1)}, bf16[288,144]{1,0:T(8,128)(2,1)}, u32[]{:S(2)}) copy-start(bf16[288,144]{1,0:T(8,128)(2,1)} %get-tuple-element.73.refs_14_.refs_20_) | copy-start | bytes 248836
  53.3 9.8 %copy-start.6 = (bf16[216,192]{1,0:T(8,128)(2,1)S(1)}, bf16[216,192]{1,0:T(8,128)(2,1)}, u32[]{:S(2)}) copy-start(bf16[216,192]{1,0:T(8,128)(2,1)} %get-tuple-element.72.refs_13_.refs_16_) | copy-start | bytes 248836
  53.3 9.8 %copy-start.13 = (f32[32,1,128]{2,1,0:T(1,128)S(1)}, f32[32,1,128]{2,1,0:T(1,128)}, u32[]{:S(2)}) copy-start(f32[32,1,128]{2,1,0:T(1,128)} %all_to_all.10.refs_2_.refs_7_) | copy-start | bytes 49156
  53.3 9.8 %collective-permute-start.5 = (f32[120,256]{1,0:T(8,128)S(1)}, f32[120,256]{1,0:T(8,128)S(1)}, u32[]{:S(2)}, u32[]{:S(2)}) collective-permute-start(f32[120,256]{1,0:T(8,128)S(1)} %get-tuple-element.70), channel_id=1, source_target_pairs={{0,29},{1,30},{2,31},{3,0},{4,1},{5,2},{6,3},{7,4},{8,5},{9,6},{10... | collective-permute-start | bytes 368648 | tf_op jit(solution)/shard_map/ppermute | solution.py:802
  77.7 10.6 %collective-permute-start.8 = (f32[64,256]{1,0:T(8,128)S(1)}, f32[64,256]{1,0:T(8,128)S(1)}, u32[]{:S(2)}, u32[]{:S(2)}) collective-permute-start(f32[64,256]{1,0:T(8,128)S(1)} %get-tuple-element.78), channel_id=1, source_target_pairs={{0,16},{1,17},{2,18},{3,19},{4,20},{5,21},{6,22},{7,23},{8,24},{9,... | collective-permute-start | bytes 196616 | tf_op jit(solution)/shard_map/ppermute | solution.py:802
  77.7 10.5 %collective-permute-start.6 = (f32[192,256]{1,0:T(8,128)S(1)}, f32[192,256]{1,0:T(8,128)S(1)}, u32[]{:S(2)}, u32[]{:S(2)}) collective-permute-start(f32[192,256]{1,0:T(8,128)S(1)} %get-tuple-element.76), channel_id=1, source_target_pairs={{0,1},{1,2},{2,3},{3,4},{4,5},{5,6},{6,7},{7,8},{8,9},{9,10},{10,1... | collective-permute-start | bytes 589832 | tf_op jit(solution)/shard_map/ppermute | solution.py:802
  77.8 10.5 %collective-permute-start.7 = (f32[192,256]{1,0:T(8,128)S(1)}, f32[192,256]{1,0:T(8,128)S(1)}, u32[]{:S(2)}, u32[]{:S(2)}) collective-permute-start(f32[192,256]{1,0:T(8,128)S(1)} %get-tuple-element.77), channel_id=1, source_target_pairs={{0,31},{1,0},{2,1},{3,2},{4,3},{5,4},{6,5},{7,6},{8,7},{9,8},{10,9... | collective-permute-start | bytes 589832 | tf_op jit(solution)/shard_map/ppermute | solution.py:802
  88.3 9.9 %collective-permute-start.9 = (f32[192,256]{1,0:T(8,128)S(1)}, f32[192,256]{1,0:T(8,128)S(1)}, u32[]{:S(2)}, u32[]{:S(2)}) collective-permute-start(f32[192,256]{1,0:T(8,128)S(1)} %get-tuple-element.88), channel_id=1, source_target_pairs={{0,3},{1,4},{2,5},{3,6},{4,7},{5,8},{6,9},{7,10},{8,11},{9,12},{10... | collective-permute-start | bytes 589832 | tf_op jit(solution)/shard_map/ppermute | solution.py:802
  88.4 9.9 %copy-start.3 = (bf16[384,1024]{1,0:T(8,128)(2,1)S(1)}, bf16[384,1024]{1,0:T(8,128)(2,1)}, u32[]{:S(2)}) copy-start(bf16[384,1024]{1,0:T(8,128)(2,1)} %get-tuple-element.50.refs_3_.own.near.refs_5_.refs_9_) | copy-start | bytes 2359300
  88.4 9.9 %copy-start.11 = (bf16[4,144,144]{2,1,0:T(8,128)(2,1)S(1)}, bf16[4,144,144]{2,1,0:T(8,128)(2,1)}, u32[]{:S(2)}) copy-start(bf16[4,144,144]{2,1,0:T(8,128)(2,1)} %get-tuple-element.53.w_lift.refs_18_) | copy-start | bytes 497668
  88.4 9.9 %copy-start.12 = (f32[9,9,3,128]{3,2,1,0:T(4,128)S(1)}, f32[9,9,3,128]{3,2,1,0:T(4,128)}, u32[]{:S(2)}) copy-start(f32[9,9,3,128]{3,2,1,0:T(4,128)} %get-tuple-element.81.refs_6_) | copy-start | bytes 373252
  88.4 9.9 %copy-start.15 = (f32[9,20,128]{2,1,0:T(8,128)S(1)}, f32[9,20,128]{2,1,0:T(8,128)}, u32[]{:S(2)}) copy-start(f32[9,20,128]{2,1,0:T(8,128)} %get-tuple-element.80.refs_5_) | copy-start | bytes 276484
  88.4 9.9 %copy-start.18 = (f32[24,128]{1,0:T(8,128)S(1)}, f32[24,128]{1,0:T(8,128)}, u32[]{:S(2)}) copy-start(f32[24,128]{1,0:T(8,128)} %get-tuple-element.82.refs_7_) | copy-start | bytes 36868
  88.5 9.9 %copy-start.19 = (s32[8,128]{1,0:T(8,128)S(1)}, s32[8,128]{1,0:T(8,128)}, u32[]{:S(2)}) copy-start(s32[8,128]{1,0:T(8,128)} %get-tuple-element.83.refs_8_) | copy-start | bytes 12292
  88.5 9.8 %collective-permute-start.10 = (f32[192,256]{1,0:T(8,128)S(1)}, f32[192,256]{1,0:T(8,128)S(1)}, u32[]{:S(2)}, u32[]{:S(2)}) collective-permute-start(f32[192,256]{1,0:T(8,128)S(1)} %get-tuple-element.89), channel_id=1, source_target_pairs={{0,29},{1,30},{2,31},{3,0},{4,1},{5,2},{6,3},{7,4},{8,5},{9,6},{10... | collective-permute-start | bytes 589832 | tf_op jit(solution)/shard_map/ppermute | solution.py:802
  (2 other events, 1.3 us)
where the time goes:
time: 115 us; the launch traced here: 114 us
  Pallas kernels  68.2 us (59%)
  starting transfers between devices  26.5 us (23%)
  blocking collectives  14.5 us (13%)
  local copies, waits for them, and re-layouts  4.74 us (4%)
    ppermute x11, starting transfers between devices, shift(): lax.ppermute(array, 'dom', [(i, (i + by) % devices) for i in range(device...  23 us
    pallas_call x4, Pallas kernels, near_steps(): pl.pallas_call(near_kernel, grid=(number,), in_specs=[spec(2 * PACK), N_S...  20.5 us
    pallas_call x1, Pallas kernels, per_device(): pl.pallas_call(last, grid=(halves + 1,), in_specs=[lane_spec(NV, NBP, las...  16 us
    pallas_call x1, Pallas kernels, per_device(): pl.pallas_call(middle, grid=(halves,), in_specs=[part_spec(0, NV, NB), pa...  14.5 us
    all_to_all x1, blocking collectives, swap(): lax.all_to_all(array, 'dom', split_axis=0, concat_axis=0, axis_index_grou...  14.5 us
    pallas_call x1, Pallas kernels, per_device(): pl.pallas_call(first_kernel, grid=(halves,), in_specs=[part_spec(0, NV, N...  11.7 us
    unnamed x44, local copies, waits for them, and re-layouts  4.74 us
    all_to_all x1, starting transfers between devices, swap(): lax.all_to_all(array, 'dom', split_axis=0, concat_axis=0, axis_index_grou...  3.43 us
  transfers between devices with their start and end apart: 12, of which 0 were waited for; matrix products, arithmetic and copies ran while one was open for 0% of the time, Pallas kernels for 28%

commit v1 on v0

--- a/solution.py
+++ b/solution.py
@@ -30,6 +30,7 @@
 RECORD = 640
 SMALL = 24
 MESSAGE1 = REQ + 8
+LIFT_AT, TABLE_AT, NEAR_ROWS = 576, 1152, 1472
 
 step_fast = 0.25
 exact = lax.Precision.HIGHEST
@@ -96,7 +97,7 @@
     return jnp.where(condition, 1.0, 0.0).astype(bf16)
 
 
-def make_weights(deriv, stiff, evals, lift, w_pred, w_own, w_lift, w_table, w_far, square):
+def make_weights(deriv, stiff, evals, lift, w_pred, w_near, w_far, square):
     def turned(matrix, rows, columns):
         square[...] = jnp.zeros((LANES, LANES), f32)
         square[:rows, :columns] = matrix
@@ -132,7 +133,7 @@
     blocks = []
     for matrix in [stiff[axis] for axis in range(3)] + own + [own[0] + own[1] + own[2] + own[3]]:
         blocks += three(matrix if len(blocks) < 9 else -0.5 * matrix)
-    w_own[...] = jnp.concatenate(blocks, axis=0).astype(bf16)
+    w_near[:LIFT_AT, :] = jnp.concatenate(blocks, axis=0).astype(bf16)
 
     column = iota((LANES, 144), 1)
     spread = one_hot(iota((LANES, 144), 0) == (column & 15))
@@ -144,7 +145,8 @@
         high, low = split(turned(lift[face], NQ, NB))
         row = jnp.where(column < 96, dot(high, spread), dot(low, spread))
         rows = [jnp.where(member == inner, -0.5 * row, 0.0) for inner in range(3)]
-        w_lift[face] = jnp.concatenate(rows + [-r for r in rows], axis=0).astype(bf16)
+        at = LIFT_AT + 144 * face
+        w_near[at : at + 144, :144] = jnp.concatenate(rows + [-r for r in rows], axis=0).astype(bf16)
         every += rows
     w_far[...] = jnp.concatenate(every, axis=0).astype(bf16)
 
@@ -154,8 +156,7 @@
     halves = []
     for part_of in split(evals[...]):
         halves.append(dot(jnp.where(keep, dot_last(basis_of, part_of), 0.0).astype(bf16), code_of))
-    w_table[:, :16] = halves[0].astype(bf16)
-    w_table[:, 16:] = halves[1].astype(bf16)
+    w_near[TABLE_AT:, :32] = jnp.concatenate(halves, axis=1).astype(bf16)
 
 
 def find_links(devices, tiles, small, aux, from_top):
@@ -501,7 +502,7 @@
     def __init__(self, near, weights, small, aux, gathered, table, by_face, parts):
         self.near, self.small, self.aux, self.gathered, self.table = near, small, aux, gathered, table
         self.by_face, self.parts = by_face, parts
-        self.w_own, self.w_lift, self.w_table = weights
+        self.weights = weights
         self.count = aux.shape[-1]
         self.tiles = range(self.count // LANES)
 
@@ -509,7 +510,7 @@
         for group in range(3):
             rows = slice(64 * group, 64 * group + 64)
             lower = slice(PACK + 64 * group, PACK + 64 * group + 64)
-            mine = dot(self.w_own[...], stacked(own[rows], own[lower]))
+            mine = dot(self.weights[:LIFT_AT, :], stacked(own[rows], own[lower]))
             for inner in range(3):
                 q = 3 * group + inner
                 of = [mine[72 * block + NBP * inner : 72 * block + NBP * inner + NBP] for block in range(8)]
@@ -526,12 +527,12 @@
         index = jnp.concatenate([index] * (KEEP // 16), axis=0)
         both = dot(self.near[...], jnp.where(slots == index, jnp.ones((), bf16), jnp.zeros((), bf16)))
         self.gathered[...] = both[:PACK] + both[PACK:]
-        self.table[...] = table_of(self.small[pl.ds(ORIENT + face, 1), :], self.w_table[...])
+        self.table[...] = table_of(self.small[pl.ds(ORIENT + face, 1), :], self.weights[TABLE_AT:, :32])
 
     def products(self, face):
         normals = [self.small[pl.ds(3 * face + d, 1), :] for d in range(3)]
         for group, points in enumerate(face_products(self.gathered, self.table, self.tiles)):
-            lifted = dot(self.w_lift[face], points)
+            lifted = dot(self.weights[pl.ds(pl.multiple_of(LIFT_AT + 144 * face, 16), 144), :144], points)
             for inner in range(3):
                 q = 3 * group + inner
                 at = inner * NBP
@@ -541,22 +542,27 @@
                     self.parts[d * NV + q] = self.parts[d * NV + q] + normals[d] * mixed
 
 
-def near_part(chains, owns):
+def near_part(chains, owns, together):
     chains[0].gather(0)
     for chain, own in zip(chains, owns):
         chain.begin(own)
 
-    def two_faces(pair, carry):
-        for face in (2 * pair, 2 * pair + 1):
+    def some_faces(step, carry):
+        for n in range(together):
+            face = step * together + n
             for other in chains[1:]:
                 other.gather(face)
             chains[0].products(face)
-            chains[0].gather((face + 1) & 3)
+            if together < 4 or n < 3:
+                chains[0].gather((face + 1) & 3)
             for other in chains[1:]:
                 other.products(face)
         return carry
 
-    lax.fori_loop(0, 2, two_faces, 0)
+    if together == 4:
+        some_faces(0, 0)
+    else:
+        lax.fori_loop(0, 4 // together, some_faces, 0)
 
 
 def update_chain(parts, far, small, aux, jac, w_far, w_table, gathered):
@@ -632,11 +638,11 @@
 
 
 def first_kernel(
-    q, jac, deriv, stiff, evals, lift, packed, slow, w_pred, w_own, w_lift, w_table, w_far, padded, sums, square
+    q, jac, deriv, stiff, evals, lift, packed, slow, w_pred, w_near, w_far, padded, sums, square
 ):
     @pl.when(pl.program_id(0) == 0)
     def _():
-        make_weights(deriv, stiff, evals, lift, w_pred, w_own, w_lift, w_table, w_far, square)
+        make_weights(deriv, stiff, evals, lift, w_pred, w_near, w_far, square)
 
     load_state(q, padded)
     chains = []
@@ -647,14 +653,14 @@
     packed[...] = split_fields(load_field(sums))
 
 
-def near_kernel(own, near, small, aux, w_own, w_lift, w_table, *refs):
+def near_kernel(own, near, small, aux, w_near, *refs):
     parts, gathered, table, by_face = refs[-4:]
     chains, owns = [], []
     for begin in range(0, BOTH, WIDE):
         windows = [Window(r, begin, WIDE) for r in (small, aux, gathered, table, by_face, parts)]
-        chains.append(NearChain(near, (w_own, w_lift, w_table), *windows))
+        chains.append(NearChain(near, w_near, *windows))
         owns.append(Window(own, begin, WIDE))
-    near_part(chains, owns)
+    near_part(chains, owns, 4)
 
 
 def middle_steps(chains, far, w_pred, w_far, w_table):
@@ -683,7 +689,7 @@
 
 def middle_kernel(devices, steps, q, jac, small, slow, parts, near, aux, asks, *refs):
     messages = refs[:5]
-    w_pred, w_far, w_table, base, packed, *outs, padded, sums, gathered, far = refs[5:]
+    w_pred, w_far, w_near, base, packed, *outs, padded, sums, gathered, far = refs[5:]
     step = pl.program_id(0)
 
     @pl.when(step == 0)
@@ -692,7 +698,7 @@
 
     refs = (q, parts, jac, small, slow, aux, gathered, base, padded, sums)
     chains = [[Window(r, begin, WIDE) for r in refs] for begin in range(0, BOTH, WIDE)]
-    second = jnp.concatenate(middle_steps(chains, far[...], w_pred, w_far[...], w_table[...]), axis=1)
+    second = jnp.concatenate(middle_steps(chains, far[...], w_pred, w_far[...], w_near[TABLE_AT:, :32]), axis=1)
     packed[:, pl.ds(pl.multiple_of(step * BOTH, BOTH), BOTH)] = second
 
     @pl.when(step == steps - 1)
@@ -704,8 +710,9 @@
     devices, steps, base, jac, small, parts, aux, q_moved, jac_moved, small_moved, aux_moved, near, later, *refs
 ):
     messages = refs[:5]
-    w_pred, w_own, w_lift, w_table, w_far, out, gathered, far = refs[5:13]
-    padded, gathered_moved, table, by_face, parts_moved, early, late, now = refs[13:]
+    w_pred, w_near, w_far, out, gathered, far = refs[5:11]
+    padded, gathered_moved, table, by_face, parts_moved, early, late, now = refs[11:]
+    w_table = w_near[TABLE_AT:, :32]
     step = pl.program_id(0)
 
     @pl.when(step == 0)
@@ -719,7 +726,7 @@
         for begin in range(0, BOTH, WIDE):
             w = [Window(r, begin, WIDE) for r in (parts, small, aux, jac, gathered, out, base)]
             chains.append(
-                update_chain(load_parts(w[0]), table_far, w[1], w[2], w[3], w_far[...], w_table[...], w[4])
+                update_chain(load_parts(w[0]), table_far, w[1], w[2], w[3], w_far[...], w_table, w[4])
             )
             stores.append((w[5], w[6], w[1]))
         for (to, start, fields), change in zip(stores, take_turns(*chains)):
@@ -730,16 +737,16 @@
         load_state(q_moved, padded)
         predict([(padded, jac_moved, [(early, FIRST), (late, SECOND)])], w_pred)
         chain = NearChain(
-            near, (w_own, w_lift, w_table), small_moved, aux_moved, gathered_moved, table, by_face, parts_moved
+            near, w_near, small_moved, aux_moved, gathered_moved, table, by_face, parts_moved
         )
-        near_part([chain], [split_fields(load_field(early))])
+        near_part([chain], [split_fields(load_field(early))], 1)
         fields = (q_moved, parts_moved, jac_moved, small_moved, late, aux_moved, gathered_moved, now, padded, early)
         far_first = far_table(devices, 1, messages)
-        (second,) = middle_steps([fields], far_first, w_pred, w_far[...], w_table[...])
+        (second,) = middle_steps([fields], far_first, w_pred, w_far[...], w_table)
         chain.near = later
-        near_part([chain], [second])
+        near_part([chain], [second], 1)
         change = update(
-            load_parts(parts_moved), far[...], small_moved, aux_moved, jac_moved, w_far[...], w_table[...],
+            load_parts(parts_moved), far[...], small_moved, aux_moved, jac_moved, w_far[...], w_table,
             gathered_moved,
         )
         store_result(out, load_field(now), change, small_moved)
@@ -831,9 +838,7 @@
     far = pltpu.VMEM((2 * PACK, FAR), bf16)
     weight_shapes = [
         jax.ShapeDtypeStruct((ROWS, PACK), bf16),
-        jax.ShapeDtypeStruct((576, PACK), bf16),
-        jax.ShapeDtypeStruct((4, 144, 144), bf16),
-        jax.ShapeDtypeStruct((320, 32), bf16),
+        jax.ShapeDtypeStruct((NEAR_ROWS, PACK), bf16),
         jax.ShapeDtypeStruct((288, 144), bf16),
     ]
     evals = jnp.transpose(face_eval, (0, 2, 1)).reshape(12 * NQ, NB)
@@ -844,7 +849,7 @@
         rank = len(lead)
         return pl.BlockSpec(lead + (BOTH,), lambda i: (0,) * rank + (i + begin,))
 
-    first, slow, w_pred, w_own, w_lift, w_table, w_far = pl.pallas_call(
+    first, slow, w_pred, w_near, w_far = pl.pallas_call(
         first_kernel,
         grid=(halves,),
         in_specs=[part_spec(0, NV, NB), part_spec(0, NV, NV, 3)] + [whole_spec(m) for m in matrices],
@@ -871,7 +876,7 @@
         compiler_params=MOST,
         name="unpack",
     )(group, one, asks, first)
-    of_near = [w_own, w_lift, w_table]
+    of_near = [w_near]
     parts_shape = jax.ShapeDtypeStruct((4 * NV, NBP, count), f32)
 
     def near_steps(field, begin, number, parts):
@@ -887,7 +892,7 @@
             out_specs=spec(4 * NV, NBP),
             out_shape=parts_shape,
             scratch_shapes=near_scratch(BOTH),
-            input_output_aliases={7: 0} if parts else {},
+            input_output_aliases={5: 0} if parts else {},
             cost_estimate=pl.CostEstimate(flops=int(4e9) * number, bytes_accessed=4 << 20, transcendentals=0),
             compiler_params=PARAMS,
             name="near",
@@ -914,7 +919,7 @@
     def middle(*refs):
         middle_kernel(devices, halves, *refs)
 
-    weights = [w_pred, w_far, w_table]
+    weights = [w_pred, w_far, w_near]
     out_shape = [field_shape, packed_shape] + message_shapes(2 * REQ)
     base, second, *answers = pl.pallas_call(
         middle,
@@ -942,7 +947,7 @@
         last_kernel(devices, halves, *refs)
 
     end = halves - 1
-    weights = [w_pred, w_own, w_lift, w_table, w_far]
+    weights = [w_pred, w_near, w_far]
     return pl.pallas_call(
         last,
         grid=(halves + 1,),

time: 115 us -> 109 us (0.948)
  Pallas kernels: 68.2 us -> 64.4 us
  local copies, waits for them, and re-layouts: 4.74 us -> 3.04 us
    pallas_call x4, Pallas kernels: 20.5 us -> 17.2 us  [near_steps(): pl.pallas_call(near_kernel, grid=(number,), in_specs=[spec(2 * PACK), N_S...]
    unnamed x44 -> x40, local copies, waits for them, and re-layouts: 4.74 us -> 3.04 us
  transfers between devices with their start and end apart: 12 -> 12, of which waited for: 0 -> 0; matrix products, arithmetic and copies ran while one was open for 0% -> 0% of each run, Pallas kernels for 28% -> 27%
where the time goes in v1:
time: 109 us
  Pallas kernels  64.4 us (59%)
  starting transfers between devices  26.5 us (24%)
  blocking collectives  14.3 us (13%)
  local copies, waits for them, and re-layouts  3.04 us (3%)
    ppermute x11, starting transfers between devices, shift(): lax.ppermute(array, 'dom', [(i, (i + by) % devices) for i in range(device...  23.1 us
    pallas_call x4, Pallas kernels, near_steps(): pl.pallas_call(near_kernel, grid=(number,), in_specs=[spec(2 * PACK), N_S...  17.2 us
    pallas_call x1, Pallas kernels, per_device(): pl.pallas_call(last, grid=(halves + 1,), in_specs=[lane_spec(NV, NBP, las...  15.5 us
    pallas_call x1, Pallas kernels, per_device(): pl.pallas_call(middle, grid=(halves,), in_specs=[part_spec(0, NV, NB), pa...  14.5 us
    all_to_all x1, blocking collectives, swap(): lax.all_to_all(array, 'dom', split_axis=0, concat_axis=0, axis_index_grou...  14.3 us
    pallas_call x1, Pallas kernels, per_device(): pl.pallas_call(first_kernel, grid=(halves,), in_specs=[part_spec(0, NV, N...  11.8 us
    all_to_all x1, starting transfers between devices, swap(): lax.all_to_all(array, 'dom', split_axis=0, concat_axis=0, axis_index_grou...  3.43 us
    unnamed x40, local copies, waits for them, and re-layouts  3.04 us
  transfers between devices with their start and end apart: 12, of which 0 were waited for; matrix products, arithmetic and copies ran while one was open for 0% of the time, Pallas kernels for 27%

profile of v1, /device:TPU:0, one launch (start us, length us, event | category | flops | bytes accessed | tf_op | source)
XLA Modules:
  0.0 108.7 jit_solution(8312416945834566816)
XLA Ops:
  0.0 2.5 %prepare.1 = (f32[24,1024]{1,0:T(8,128)}, s32[8,1024]{1,0:T(8,128)}, f32[32,1,128]{2,1,0:T(1,128)}, f32[8,16,640]{2,1,0:T(8,128)}, f32[16,640]{1,0:T(8,128)}) custom-call(f32[3,4,1024]{2,1,0:T(4,128)} %bitcast.13, f32[1,1024]{1,0:T(1,128)} %bitcast.14, s32[1,1024]{1,0:T(1,128)} %bitcast.15, s32[1,1024]{1,0:T(1,128)} %bitcast.16, s32[4,1024]{1,0:T(4,128)} %refs_4_.1, ...), custom_call_target="tpu_custom_call" | custom-call | tf_op jit(solution)/shard_map/prepare/pallas_call | solution.py:243
  2.5 14.3 %all_to_all.10.refs_2_.refs_7_ = f32[32,1,128]{2,1,0:T(1,128)} all-to-all(f32[32,1,128]{2,1,0:T(1,128)} %get-tuple-element.51), channel_id=1, replica_groups=mesh['dom'=32] {'dom'}, dimensions={0} | all-to-all | bytes 32768 | tf_op jit(solution)/shard_map/all_to_all | solution.py:812
  16.9 3.4 %all-to-all-start.1 = ((f32[8,16,640]{2,1,0:T(8,128)}), f32[8,16,640]{2,1,0:T(8,128)S(1)}, u32[]{:S(2)}, u32[]{:S(2)}) async-start(f32[8,16,640]{2,1,0:T(8,128)} %get-tuple-element.54), calls=%async_computation.1 | async-start | bytes 655360 | tf_op jit(solution)/shard_map/all_to_all | solution.py:812
  20.3 0.1 collective-permute-start
  20.4 11.8 %first.1 = (bf16[384,1024]{1,0:T(8,128)(2,1)}, f32[9,24,1024]{2,1,0:T(8,128)}, bf16[216,192]{1,0:T(8,128)(2,1)}, bf16[1472,192]{1,0:T(8,128)(2,1)}, bf16[288,144]{1,0:T(8,128)(2,1)}) custom-call(f32[9,20,1024]{2,1,0:T(8,128)} %refs_0_.1, f32[9,9,3,1024]{3,2,1,0:T(4,128)} %bitcast.9, f32[3,20,20]{2,1,0:T(8,128)} %deriv.1, f32[3,20,20]{2,1,0:T(8,128)} %stiff.1, ...), custom_call_target="tpu_custom_call" | custom-call | tf_op jit(solution)/shard_map/first/pallas_call | solution.py:852
  32.2 0.0 collective-permute-done.refs_1_
  32.2 0.0 all-to-all-done.1.refs_0_
  32.2 0.6 copy-done.19
  32.8 0.1 copy-done.18
  32.9 2.9 %unpack.1 = (f32[9,20,128]{2,1,0:T(8,128)}, f32[9,9,3,128]{3,2,1,0:T(4,128)}, f32[24,128]{1,0:T(8,128)}, s32[8,128]{1,0:T(8,128)}, f32[120,256]{1,0:T(8,128)}, /...) custom-call(f32[8,16,640]{2,1,0:T(8,128)} %copy-done.18, f32[16,640]{1,0:T(8,128)} %copy-done.19, ...), custom_call_target="tpu_custom_call" | custom-call | tf_op jit(solution)/shard_map/unpack/pallas_call | solution.py:870
  35.8 2.8 %collective-permute-start.3 = (f32[40,256]{1,0:T(8,128)}, f32[40,256]{1,0:T(8,128)S(1)}, u32[]{:S(2)}, u32[]{:S(2)}) collective-permute-start(f32[40,256]{1,0:T(8,128)} %get-tuple-element.59), channel_id=1, source_target_pairs={{0,16},{1,17},{2,18},{3,19},{4,20},{5,21},{6,22},{7,23},{8,24},{9,... | collective-permute-start | bytes 122888 | tf_op jit(solution)/shard_map/ppermute | solution.py:809
  38.5 0.5 collective-permute-start.1
  39.0 4.9 %collective-permute-start.2 = (f32[120,256]{1,0:T(8,128)}, f32[120,256]{1,0:T(8,128)S(1)}, u32[]{:S(2)}, u32[]{:S(2)}) collective-permute-start(f32[120,256]{1,0:T(8,128)} %get-tuple-element.58), channel_id=1, source_target_pairs={{0,31},{1,0},{2,1},{3,2},{4,3},{5,4},{6,5},{7,6},{8,7},{9,8},{10,9... | collective-permute-start | bytes 368648 | tf_op jit(solution)/shard_map/ppermute | solution.py:809
  43.9 1.1 %copy-done.2 = bf16[384,1024]{1,0:T(8,128)(2,1)S(1)} copy-done((bf16[384,1024]{1,0:T(8,128)(2,1)S(1)}, bf16[384,1024]{1,0:T(8,128)(2,1)}, u32[]{:S(2)}) %copy-start.2) | copy-done | bytes 786456
  45.0 1.1 %copy-done.4 = bf16[1472,192]{1,0:T(8,128)(2,1)S(1)} copy-done((bf16[1472,192]{1,0:T(8,128)(2,1)S(1)}, bf16[1472,192]{1,0:T(8,128)(2,1)}, u32[]{:S(2)}) %copy-start.4) | copy-done | bytes 565272
  46.1 4.3 %near.4.refs_0_ = f32[36,24,1024]{2,1,0:T(8,128)S(1)} custom-call(bf16[384,1024]{1,0:T(8,128)(2,1)S(1)} %copy-done.2, bf16[384,1024]{1,0:T(8,128)(2,1)S(1)} %copy-done.2, f32[24,1024]{1,0:T(8,128)S(1)} %copy-done.9, s32[8,1024]{1,0:T(8,128)S(1)} %copy-done.12, bf16[1472,192]{1,0:T(8,128)(2,1)S(1)} %copy-done.4), custom_call_target="tpu_custom_call" | custom-call | flops 4000000000 | bytes 4194304 | tf_op jit(solution)/shard_map/near/pallas_call | solution.py:886
  50.5 0.0 collective-permute-done.1.got_plus.refs_8_
  50.5 0.1 collective-permute-start.4
  50.6 0.0 copy-start
  50.6 0.0 copy-start.1
  50.6 0.0 copy-start.6
  50.7 4.6 %collective-permute-start.5 = (f32[120,256]{1,0:T(8,128)S(1)}, f32[120,256]{1,0:T(8,128)S(1)}, u32[]{:S(2)}, u32[]{:S(2)}) collective-permute-start(f32[120,256]{1,0:T(8,128)S(1)} %get-tuple-element.66), channel_id=1, source_target_pairs={{0,29},{1,30},{2,31},{3,0},{4,1},{5,2},{6,3},{7,4},{8,5},{9,6},{10... | collective-permute-start | bytes 368648 | tf_op jit(solution)/shard_map/ppermute | solution.py:809
  55.3 4.3 %near.5.refs_4_ = f32[36,24,1024]{2,1,0:T(8,128)S(1)} custom-call(bf16[384,1024]{1,0:T(8,128)(2,1)S(1)} %copy-done.2, bf16[384,1024]{1,0:T(8,128)(2,1)S(1)} %copy-done.2, f32[24,1024]{1,0:T(8,128)S(1)} %copy-done.9, s32[8,1024]{1,0:T(8,128)S(1)} %copy-done.12, bf16[1472,192]{1,0:T(8,128)(2,1)S(1)} %copy-done.4, ...), custom_call_target="tpu_custom_call", output_to_operand_aliasing={{}: (5, {})} | custom-call | flops 4000000000 | bytes 4194304 | tf_op jit(solution)/shard_map/near/pallas_call | solution.py:886
  59.7 14.5 %middle.1 = (f32[9,24,1024]{2,1,0:T(8,128)S(1)}, bf16[384,1024]{1,0:T(8,128)(2,1)S(1)}, f32[192,256]{1,0:T(8,128)S(1)}, f32[192,256]{1,0:T(8,128)S(1)}, f32[64,2...) custom-call(f32[9,20,1024]{2,1,0:T(8,128)S(1)} %copy-done.1, f32[9,9,3,1024]{3,2,1,0:T(4,128)S(1)} %bitcast.10, ...), custom_call_target="tpu_custom_call" | custom-call | tf_op jit(solution)/shard_map/middle/pallas_call | solution.py:924
  74.2 0.1 collective-permute-start.8
  74.3 0.1 collective-permute-start.6
  74.3 5.3 %collective-permute-start.7 = (f32[192,256]{1,0:T(8,128)S(1)}, f32[192,256]{1,0:T(8,128)S(1)}, u32[]{:S(2)}, u32[]{:S(2)}) collective-permute-start(f32[192,256]{1,0:T(8,128)S(1)} %get-tuple-element.73), channel_id=1, source_target_pairs={{0,31},{1,0},{2,1},{3,2},{4,3},{5,4},{6,5},{7,6},{8,7},{9,8},{10,9... | collective-permute-start | bytes 589832 | tf_op jit(solution)/shard_map/ppermute | solution.py:809
  79.7 4.3 %near.6.refs_0_ = f32[36,24,1024]{2,1,0:T(8,128)S(1)} custom-call(bf16[384,1024]{1,0:T(8,128)(2,1)S(1)} %get-tuple-element.71.own.near.refs_10_, bf16[384,1024]{1,0:T(8,128)(2,1)S(1)} %get-tuple-element.71.own.near.refs_10_, f32[24,1024]{1,0:T(8,128)S(1)} %copy-done.9, s32[8,1024]{1,0:T(8,128)S(1)} %copy-done.12, bf16[1472,192]{1,0:T(8,128)(2,1)S(1)} %copy-done.5), custom_call_target="tpu_custom_call" | custom-call | flops 4000000000 | bytes 4194304 | tf_op jit(solution)/shard_map/near/pallas_call | solution.py:886
  84.0 0.1 collective-permute-start.9
  84.2 4.7 %collective-permute-start.10 = (f32[192,256]{1,0:T(8,128)S(1)}, f32[192,256]{1,0:T(8,128)S(1)}, u32[]{:S(2)}, u32[]{:S(2)}) collective-permute-start(f32[192,256]{1,0:T(8,128)S(1)} %get-tuple-element.85), channel_id=1, source_target_pairs={{0,29},{1,30},{2,31},{3,0},{4,1},{5,2},{6,3},{7,4},{8,5},{9,6},{10... | collective-permute-start | bytes 589832 | tf_op jit(solution)/shard_map/ppermute | solution.py:809
  88.8 4.3 %near.7.refs_3_ = f32[36,24,1024]{2,1,0:T(8,128)S(1)} custom-call(bf16[384,1024]{1,0:T(8,128)(2,1)S(1)} %get-tuple-element.71.own.near.refs_10_, bf16[384,1024]{1,0:T(8,128)(2,1)S(1)} %get-tuple-element.71.own.near.refs_10_, f32[24,1024]{1,0:T(8,128)S(1)} %copy-done.9, s32[8,1024]{1,0:T(8,128)S(1)} %copy-done.12, ...), custom_call_target="tpu_custom_call", output_to_operand_aliasing={{}: (5, {})} | custom-call | flops 4000000000 | bytes 4194304 | tf_op jit(solution)/shard_map/near/pallas_call | solution.py:886
  93.2 15.5 %last.1 = f32[9,20,1152]{2,1,0:T(8,128)} custom-call(f32[9,24,1024]{2,1,0:T(8,128)S(1)} %get-tuple-element.70.refs_0_, f32[9,9,3,1024]{3,2,1,0:T(4,128)S(1)} %bitcast.11, f32[24,1024]{1,0:T(8,128)S(1)} %copy-done.9, f32[36,24,1024]{2,1,0:T(8,128)S(1)} %near.7.refs_3_, s32[8,1024]{1,0:T(8,128)S(1)} %copy-done.12, f32[9,20,128]{2,1,0:T(8,128)S(1)} %copy-done.13, ...), custom_call_target="tpu_custom_call" | custom-call | tf_op jit(solution)/shard_map/last/pallas_call | solution.py:951
  (44 shorter events, 0.1 us)
Async XLA Ops:
  2.5 41.4 %copy-start.9 = (f32[24,1024]{1,0:T(8,128)S(1)}, f32[24,1024]{1,0:T(8,128)}, u32[]{:S(2)}) copy-start(f32[24,1024]{1,0:T(8,128)} %get-tuple-element.46.small.refs_2_) | copy-start | bytes 294916
  2.5 41.4 %copy-start.12 = (s32[8,1024]{1,0:T(8,128)S(1)}, s32[8,1024]{1,0:T(8,128)}, u32[]{:S(2)}) copy-start(s32[8,1024]{1,0:T(8,128)} %get-tuple-element.49.aux.refs_6_.refs_4_) | copy-start | bytes 98308
  16.9 15.3 %all-to-all-start.1 = ((f32[8,16,640]{2,1,0:T(8,128)}), f32[8,16,640]{2,1,0:T(8,128)S(1)}, u32[]{:S(2)}, u32[]{:S(2)}) async-start(f32[8,16,640]{2,1,0:T(8,128)} %get-tuple-element.54), calls=%async_computation.1 | async-start | bytes 655360 | tf_op jit(solution)/shard_map/all_to_all | solution.py:812
  20.3 11.9 %collective-permute-start = (f32[16,640]{1,0:T(8,128)}, f32[16,640]{1,0:T(8,128)S(1)}, u32[]{:S(2)}, u32[]{:S(2)}) collective-permute-start(f32[16,640]{1,0:T(8,128)} %get-tuple-element.55), channel_id=1, source_target_pairs={{0,1},{1,2},{2,3},{3,4},{4,5},{5,6},{6,7},{7,8},{8,9},{9,10},{10,1... | collective-permute-start | bytes 122888 | tf_op jit(solution)/shard_map/ppermute | solution.py:809
  32.2 0.6 copy-start.19
  32.2 0.7 copy-start.18
  35.8 14.7 %collective-permute-start.3 = (f32[40,256]{1,0:T(8,128)}, f32[40,256]{1,0:T(8,128)S(1)}, u32[]{:S(2)}, u32[]{:S(2)}) collective-permute-start(f32[40,256]{1,0:T(8,128)} %get-tuple-element.59), channel_id=1, source_target_pairs={{0,16},{1,17},{2,18},{3,19},{4,20},{5,21},{6,22},{7,23},{8,24},{9,... | collective-permute-start | bytes 122888 | tf_op jit(solution)/shard_map/ppermute | solution.py:809
  38.5 11.9 %collective-permute-start.1 = (f32[120,256]{1,0:T(8,128)}, f32[120,256]{1,0:T(8,128)S(1)}, u32[]{:S(2)}, u32[]{:S(2)}) collective-permute-start(f32[120,256]{1,0:T(8,128)} %get-tuple-element.57), channel_id=1, source_target_pairs={{0,1},{1,2},{2,3},{3,4},{4,5},{5,6},{6,7},{7,8},{8,9},{9,10},{10,1... | collective-permute-start | bytes 368648 | tf_op jit(solution)/shard_map/ppermute | solution.py:809
  39.0 11.5 %collective-permute-start.2 = (f32[120,256]{1,0:T(8,128)}, f32[120,256]{1,0:T(8,128)S(1)}, u32[]{:S(2)}, u32[]{:S(2)}) collective-permute-start(f32[120,256]{1,0:T(8,128)} %get-tuple-element.58), channel_id=1, source_target_pairs={{0,31},{1,0},{2,1},{3,2},{4,3},{5,4},{6,5},{7,6},{8,7},{9,8},{10,9... | collective-permute-start | bytes 368648 | tf_op jit(solution)/shard_map/ppermute | solution.py:809
  43.9 1.1 %copy-start.2 = (bf16[384,1024]{1,0:T(8,128)(2,1)S(1)}, bf16[384,1024]{1,0:T(8,128)(2,1)}, u32[]{:S(2)}) copy-start(bf16[384,1024]{1,0:T(8,128)(2,1)} %get-tuple-element.48.refs_3_.own.near.refs_5_.refs_9_) | copy-start | bytes 2359300
  45.0 1.1 %copy-start.4 = (bf16[1472,192]{1,0:T(8,128)(2,1)S(1)}, bf16[1472,192]{1,0:T(8,128)(2,1)}, u32[]{:S(2)}) copy-start(bf16[1472,192]{1,0:T(8,128)(2,1)} %get-tuple-element.50.w_near.refs_15_.refs_17_) | copy-start | bytes 1695748
  46.1 4.3 %copy-start.14 = (f32[40,256]{1,0:T(8,128)S(1)}, f32[40,256]{1,0:T(8,128)}, u32[]{:S(2)}) copy-start(f32[40,256]{1,0:T(8,128)} %get-tuple-element.63.own_plus) | copy-start | bytes 122884
  46.1 4.4 %copy-start.15 = (f32[40,256]{1,0:T(8,128)S(1)}, f32[40,256]{1,0:T(8,128)}, u32[]{:S(2)}) copy-start(f32[40,256]{1,0:T(8,128)} %get-tuple-element.64.own_minus) | copy-start | bytes 122884
  50.5 9.1 %collective-permute-start.4 = (f32[120,256]{1,0:T(8,128)S(1)}, f32[120,256]{1,0:T(8,128)S(1)}, u32[]{:S(2)}, u32[]{:S(2)}) collective-permute-start(f32[120,256]{1,0:T(8,128)S(1)} %get-tuple-element.65), channel_id=1, source_target_pairs={{0,3},{1,4},{2,5},{3,6},{4,7},{5,8},{6,9},{7,10},{8,11},{9,12},{10... | collective-permute-start | bytes 368648 | tf_op jit(solution)/shard_map/ppermute | solution.py:809
  50.6 9.0 %copy-start = (f32[3,9,9,1024]{3,0,2,1:T(4,128)S(1)}, f32[3,9,9,1024]{3,0,2,1:T(4,128)}, u32[]{:S(2)}) copy-start(f32[3,9,9,1024]{3,0,2,1:T(4,128)} %param.13) | copy-start | bytes 2985988
  50.6 9.0 %copy-start.1 = (f32[9,20,1024]{2,1,0:T(8,128)S(1)}, f32[9,20,1024]{2,1,0:T(8,128)}, u32[]{:S(2)}) copy-start(f32[9,20,1024]{2,1,0:T(8,128)} %refs_0_.1) | copy-start | bytes 2211844
  50.6 9.0 %copy-start.6 = (f32[9,24,1024]{2,1,0:T(8,128)S(1)}, f32[9,24,1024]{2,1,0:T(8,128)}, u32[]{:S(2)}) copy-start(f32[9,24,1024]{2,1,0:T(8,128)} %get-tuple-element.47.refs_3_) | copy-start | bytes 2654212
  50.6 9.0 %copy-start.7 = (bf16[288,144]{1,0:T(8,128)(2,1)S(1)}, bf16[288,144]{1,0:T(8,128)(2,1)}, u32[]{:S(2)}) copy-start(bf16[288,144]{1,0:T(8,128)(2,1)} %get-tuple-element.69.refs_14_.refs_18_) | copy-start | bytes 248836
  50.6 9.0 %copy-start.8 = (bf16[216,192]{1,0:T(8,128)(2,1)S(1)}, bf16[216,192]{1,0:T(8,128)(2,1)}, u32[]{:S(2)}) copy-start(bf16[216,192]{1,0:T(8,128)(2,1)} %get-tuple-element.68.refs_13_.refs_16_) | copy-start | bytes 248836
  50.7 9.0 %copy-start.11 = (f32[32,1,128]{2,1,0:T(1,128)S(1)}, f32[32,1,128]{2,1,0:T(1,128)}, u32[]{:S(2)}) copy-start(f32[32,1,128]{2,1,0:T(1,128)} %all_to_all.10.refs_2_.refs_7_) | copy-start | bytes 49156
  50.7 8.9 %collective-permute-start.5 = (f32[120,256]{1,0:T(8,128)S(1)}, f32[120,256]{1,0:T(8,128)S(1)}, u32[]{:S(2)}, u32[]{:S(2)}) collective-permute-start(f32[120,256]{1,0:T(8,128)S(1)} %get-tuple-element.66), channel_id=1, source_target_pairs={{0,29},{1,30},{2,31},{3,0},{4,1},{5,2},{6,3},{7,4},{8,5},{9,6},{10... | collective-permute-start | bytes 368648 | tf_op jit(solution)/shard_map/ppermute | solution.py:809
  59.7 20.0 %copy-start.5 = (bf16[1472,192]{1,0:T(8,128)(2,1)S(1)}, bf16[1472,192]{1,0:T(8,128)(2,1)}, u32[]{:S(2)}) copy-start(bf16[1472,192]{1,0:T(8,128)(2,1)} %get-tuple-element.50.w_near.refs_15_.refs_17_) | copy-start | bytes 1695748
  74.2 9.8 %collective-permute-start.8 = (f32[64,256]{1,0:T(8,128)S(1)}, f32[64,256]{1,0:T(8,128)S(1)}, u32[]{:S(2)}, u32[]{:S(2)}) collective-permute-start(f32[64,256]{1,0:T(8,128)S(1)} %get-tuple-element.74), channel_id=1, source_target_pairs={{0,16},{1,17},{2,18},{3,19},{4,20},{5,21},{6,22},{7,23},{8,24},{9,... | collective-permute-start | bytes 196616 | tf_op jit(solution)/shard_map/ppermute | solution.py:809
  74.3 9.7 %collective-permute-start.6 = (f32[192,256]{1,0:T(8,128)S(1)}, f32[192,256]{1,0:T(8,128)S(1)}, u32[]{:S(2)}, u32[]{:S(2)}) collective-permute-start(f32[192,256]{1,0:T(8,128)S(1)} %get-tuple-element.72), channel_id=1, source_target_pairs={{0,1},{1,2},{2,3},{3,4},{4,5},{5,6},{6,7},{7,8},{8,9},{9,10},{10,1... | collective-permute-start | bytes 589832 | tf_op jit(solution)/shard_map/ppermute | solution.py:809
  74.3 9.7 %collective-permute-start.7 = (f32[192,256]{1,0:T(8,128)S(1)}, f32[192,256]{1,0:T(8,128)S(1)}, u32[]{:S(2)}, u32[]{:S(2)}) collective-permute-start(f32[192,256]{1,0:T(8,128)S(1)} %get-tuple-element.73), channel_id=1, source_target_pairs={{0,31},{1,0},{2,1},{3,2},{4,3},{5,4},{6,5},{7,6},{8,7},{9,8},{10,9... | collective-permute-start | bytes 589832 | tf_op jit(solution)/shard_map/ppermute | solution.py:809
  84.0 9.1 %collective-permute-start.9 = (f32[192,256]{1,0:T(8,128)S(1)}, f32[192,256]{1,0:T(8,128)S(1)}, u32[]{:S(2)}, u32[]{:S(2)}) collective-permute-start(f32[192,256]{1,0:T(8,128)S(1)} %get-tuple-element.84), channel_id=1, source_target_pairs={{0,3},{1,4},{2,5},{3,6},{4,7},{5,8},{6,9},{7,10},{8,11},{9,12},{10... | collective-permute-start | bytes 589832 | tf_op jit(solution)/shard_map/ppermute | solution.py:809
  84.1 9.1 %copy-start.3 = (bf16[384,1024]{1,0:T(8,128)(2,1)S(1)}, bf16[384,1024]{1,0:T(8,128)(2,1)}, u32[]{:S(2)}) copy-start(bf16[384,1024]{1,0:T(8,128)(2,1)} %get-tuple-element.48.refs_3_.own.near.refs_5_.refs_9_) | copy-start | bytes 2359300
  84.1 9.1 %copy-start.10 = (f32[9,9,3,128]{3,2,1,0:T(4,128)S(1)}, f32[9,9,3,128]{3,2,1,0:T(4,128)}, u32[]{:S(2)}) copy-start(f32[9,9,3,128]{3,2,1,0:T(4,128)} %get-tuple-element.77.refs_6_) | copy-start | bytes 373252
  84.1 9.1 %copy-start.13 = (f32[9,20,128]{2,1,0:T(8,128)S(1)}, f32[9,20,128]{2,1,0:T(8,128)}, u32[]{:S(2)}) copy-start(f32[9,20,128]{2,1,0:T(8,128)} %get-tuple-element.76.refs_5_) | copy-start | bytes 276484
  84.1 9.1 %copy-start.16 = (f32[24,128]{1,0:T(8,128)S(1)}, f32[24,128]{1,0:T(8,128)}, u32[]{:S(2)}) copy-start(f32[24,128]{1,0:T(8,128)} %get-tuple-element.78.refs_7_) | copy-start | bytes 36868
  84.2 9.1 %copy-start.17 = (s32[8,128]{1,0:T(8,128)S(1)}, s32[8,128]{1,0:T(8,128)}, u32[]{:S(2)}) copy-start(s32[8,128]{1,0:T(8,128)} %get-tuple-element.79.refs_8_) | copy-start | bytes 12292
  84.2 9.0 %collective-permute-start.10 = (f32[192,256]{1,0:T(8,128)S(1)}, f32[192,256]{1,0:T(8,128)S(1)}, u32[]{:S(2)}, u32[]{:S(2)}) collective-permute-start(f32[192,256]{1,0:T(8,128)S(1)} %get-tuple-element.85), channel_id=1, source_target_pairs={{0,29},{1,30},{2,31},{3,0},{4,1},{5,2},{6,3},{7,4},{8,5},{9,6},{10... | collective-permute-start | bytes 589832 | tf_op jit(solution)/shard_map/ppermute | solution.py:809
